TPU v7x, 32 devices: a whole 2x2x4 slice. The times are simulated.
32 devices in a mesh: dp: 32 (over z, y, x, core).
Axes of the slice: x: 2, y: 2, z: 4, core: 2. Of those that a mesh axis runs over, the one named last changes fastest.
Arguments:
- tokens: bfloat16 [4096, 768], P('dp'), may hold values from -6 to 6
- lengths: int32 [64], P('dp'), may hold values from 0 to 128, as said below
- qkv_weight: bfloat16 [768, 2304], P('dp'), may hold values from -0.21875 to 0.21875
- query_bias: bfloat16 [768], P('dp'), may hold values from -3 to 3
- value_bias: bfloat16 [768], P('dp'), may hold values from -3 to 3
- out_weight: bfloat16 [768, 768], P('dp'), may hold values from -0.875 to 0.875
- out_bias: bfloat16 [768], P('dp'), may hold values from -3 to 3
- norm_one_gain: bfloat16 [768], P('dp'), may hold values from 0.5 to 1.5
- norm_one_shift: bfloat16 [768], P('dp'), may hold values from -3 to 3
- ff_in_weight: bfloat16 [768, 3072], P('dp'), may hold values from -0.21875 to 0.21875
- ff_in_bias: bfloat16 [3072], P('dp'), may hold values from -3 to 3
- ff_out_weight: bfloat16 [3072, 768], P('dp'), may hold values from -0.109375 to 0.109375
- ff_out_bias: bfloat16 [768], P('dp'), may hold values from -3 to 3
- norm_two_gain: bfloat16 [768], P('dp'), may hold values from 0.5 to 1.5
- norm_two_shift: bfloat16 [768], P('dp'), may hold values from -3 to 3
- out_grad: bfloat16 [4096, 768], P('dp'), may hold values from -6 to 6
Outputs:
- encoded: bfloat16 [4096, 768], P('dp')
- grad_tokens: float32 [4096, 768], P('dp')
- grad_qkv_weight: float32 [768, 2304], P('dp')
- grad_query_bias: float32 [768], P('dp')
- grad_value_bias: float32 [768], P('dp')
- grad_out_weight: float32 [768, 768], P('dp')
- grad_out_bias: float32 [768], P('dp')
- grad_norm_one_gain: float32 [768], P('dp')
- grad_norm_one_shift: float32 [768], P('dp')
- grad_ff_in_weight: float32 [768, 3072], P('dp')
- grad_ff_in_bias: float32 [3072], P('dp')
- grad_ff_out_weight: float32 [3072, 768], P('dp')
- grad_ff_out_bias: float32 [768], P('dp')
- grad_norm_two_gain: float32 [768], P('dp')
- grad_norm_two_shift: float32 [768], P('dp')
Inputs may be any that keep to these rules, and one draw needn't show every extreme that they name: Each device's 2 lengths sum to at most 128; its tokens are its sequences in slot order, then padding. In every draw some device holds one sequence of 128 tokens and a second slot of 0.
All inputs are finite; a program needn't handle non-finite values.
Results may differ from a plain program's by a relative error of at most 0.015.
Values may be sent and summed in bfloat16 or wider, within the bound.
A program may use at most 192 MiB of HBM per device.

v0:
```python
import jax
import jax.numpy as jnp
from jax import lax
from jax.sharding import PartitionSpec as P

HEAD_DIM = 64


def layer_norm(hidden, gain, shift):
    center = jnp.mean(hidden, axis=-1, keepdims=True)
    centered = hidden - center
    spread = jnp.mean(centered * centered, axis=-1, keepdims=True)
    return centered * lax.rsqrt(spread + 1e-06) * gain + shift


def gelu_exact(values):
    return jax.nn.gelu(values, approximate=False)


def to_low(values):
    return values.astype(jnp.bfloat16)


def as_float(values):
    return values.astype(jnp.float32)


def matmul(left, right):
    return jnp.dot(left, right, preferred_element_type=jnp.float32)


def matmul_left_t(left, right):
    return lax.dot_general(
        left, right, (((0,), (0,)), ((), ())), preferred_element_type=jnp.float32
    )


def matmul_right_t(left, right):
    return lax.dot_general(
        left, right, (((1,), (1,)), ((), ())), preferred_element_type=jnp.float32
    )


def masked_scores(queries, keys, allowed):
    raw = jnp.einsum(
        "hqd,hkd->hqk", queries, keys, preferred_element_type=jnp.float32
    ) * HEAD_DIM ** (-0.5)
    return jnp.where(allowed[None], raw, -1e30)


def by_owner(gradients, devices):
    return tuple((g.reshape(devices, -1) for g in gradients))


def body(
    tokens,
    lengths,
    qkv_weight,
    query_bias,
    value_bias,
    out_weight,
    out_bias,
    norm_one_gain,
    norm_one_shift,
    ff_in_weight,
    ff_in_bias,
    ff_out_weight,
    ff_out_bias,
    norm_two_gain,
    norm_two_shift,
    out_grad,
):
    rows, width = tokens.shape
    heads = width // HEAD_DIM
    scale = HEAD_DIM ** (-0.5)
    devices = lax.axis_size("dp")
    shard_shapes = (
        qkv_weight.shape,
        query_bias.shape,
        value_bias.shape,
        out_weight.shape,
        out_bias.shape,
        norm_one_gain.shape,
        norm_one_shift.shape,
        ff_in_weight.shape,
        ff_in_bias.shape,
        ff_out_weight.shape,
        ff_out_bias.shape,
        norm_two_gain.shape,
        norm_two_shift.shape,
    )
    attn_full = (
        lax.all_gather(qkv_weight, "dp", axis=0, tiled=True),
        lax.all_gather(query_bias, "dp", axis=0, tiled=True),
        lax.all_gather(value_bias, "dp", axis=0, tiled=True),
        lax.all_gather(out_weight, "dp", axis=0, tiled=True),
        lax.all_gather(out_bias, "dp", axis=0, tiled=True),
        lax.all_gather(norm_one_gain, "dp", axis=0, tiled=True),
        lax.all_gather(norm_one_shift, "dp", axis=0, tiled=True),
    )
    ffn_full = (
        lax.all_gather(ff_in_weight, "dp", axis=0, tiled=True),
        lax.all_gather(ff_in_bias, "dp", axis=0, tiled=True),
        lax.all_gather(ff_out_weight, "dp", axis=0, tiled=True),
        lax.all_gather(ff_out_bias, "dp", axis=0, tiled=True),
        lax.all_gather(norm_two_gain, "dp", axis=0, tiled=True),
        lax.all_gather(norm_two_shift, "dp", axis=0, tiled=True),
    )
    weight_qkv, bias_query, bias_value, weight_out, bias_out, gain_first, shift_first = attn_full
    weight_in, bias_in, weight_down, bias_down, gain_second, shift_second = ffn_full
    bounds = jnp.cumsum(lengths)
    position = jnp.arange(rows, dtype=jnp.int32)
    segments = jnp.sum((position[:, None] >= bounds[None, :]).astype(jnp.int32), axis=1)
    allowed = segments[:, None] == segments[None, :]
    zero_keys = jnp.zeros((width,), jnp.float32)
    qkv_bias = jnp.concatenate([as_float(bias_query), zero_keys, as_float(bias_value)])
    projected = to_low(matmul(tokens, weight_qkv) + qkv_bias)
    split = projected.reshape(rows, 3, heads, HEAD_DIM).transpose(1, 2, 0, 3)
    queries, keys, values = (split[0], split[1], split[2])
    scores = masked_scores(queries, keys, allowed)
    peak = jnp.max(scores, axis=-1, keepdims=True)
    log_total = peak + jnp.log(jnp.sum(jnp.exp(scores - peak), axis=-1, keepdims=True))
    attend = jnp.exp(scores - log_total)
    context = jnp.einsum("hqk,hkd->qhd", to_low(attend), values, preferred_element_type=jnp.float32)
    context = to_low(context.reshape(rows, width))
    first_sum = as_float(tokens) + matmul(context, weight_out) + as_float(bias_out)
    first_norm, norm_one_pull = jax.vjp(
        layer_norm, first_sum, as_float(gain_first), as_float(shift_first)
    )
    first_low = to_low(first_norm)
    pre_act = matmul(first_low, weight_in) + as_float(bias_in)
    activated = to_low(gelu_exact(pre_act))
    second_sum = first_norm + matmul(activated, weight_down) + as_float(bias_down)
    encoded, norm_two_pull = jax.vjp(
        layer_norm, second_sum, as_float(gain_second), as_float(shift_second)
    )
    back_weight_in = ffn_full[0]
    back_weight_down = ffn_full[2]
    grad_second, grad_gain_second, grad_shift_second = norm_two_pull(as_float(out_grad))
    grad_ff = to_low(grad_second)
    grad_weight_down = matmul_left_t(activated, grad_ff)
    grad_bias_down = jnp.sum(as_float(grad_ff), axis=0)
    grad_act = matmul_right_t(grad_ff, back_weight_down)
    gelu_pull = jax.vjp(gelu_exact, pre_act)[1]
    grad_pre = to_low(gelu_pull(grad_act)[0])
    grad_weight_in = matmul_left_t(first_low, grad_pre)
    grad_bias_in = jnp.sum(as_float(grad_pre), axis=0)
    grad_first = grad_second + matmul_right_t(grad_pre, back_weight_in)
    back_weight_qkv = attn_full[0]
    back_weight_out = attn_full[3]
    grad_first_sum, grad_gain_first, grad_shift_first = norm_one_pull(grad_first)
    grad_attn = to_low(grad_first_sum)
    grad_weight_out = matmul_left_t(context, grad_attn)
    grad_bias_out = jnp.sum(as_float(grad_attn), axis=0)
    grad_context = to_low(matmul_right_t(grad_attn, back_weight_out))
    grad_heads = grad_context.reshape(rows, heads, HEAD_DIM).transpose(1, 0, 2)
    again_scores = masked_scores(queries, keys, allowed)
    again_attend = jnp.exp(again_scores - log_total)
    grad_values = jnp.einsum(
        "hqk,hqd->hkd", to_low(again_attend), grad_heads, preferred_element_type=jnp.float32
    )
    grad_attend = jnp.einsum("hqd,hkd->hqk", grad_heads, values, preferred_element_type=jnp.float32)
    row_total = jnp.sum(grad_attend * again_attend, axis=-1, keepdims=True)
    grad_scores = to_low(again_attend * (grad_attend - row_total))
    grad_queries = (
        jnp.einsum("hqk,hkd->hqd", grad_scores, keys, preferred_element_type=jnp.float32) * scale
    )
    grad_keys = (
        jnp.einsum("hqk,hqd->hkd", grad_scores, queries, preferred_element_type=jnp.float32) * scale
    )
    grad_qkv = to_low(
        jnp.stack([grad_queries, grad_keys, grad_values])
        .transpose(2, 0, 1, 3)
        .reshape(rows, 3 * width)
    )
    grad_weight_qkv = matmul_left_t(tokens, grad_qkv)
    grad_columns = jnp.sum(as_float(grad_qkv), axis=0)
    grad_bias_query = grad_columns[:width]
    grad_bias_value = grad_columns[2 * width :]
    grad_tokens = grad_first_sum + matmul_right_t(grad_qkv, back_weight_qkv)
    all_flat = by_owner(
        (
            grad_weight_qkv,
            grad_bias_query,
            grad_bias_value,
            grad_weight_out,
            grad_bias_out,
            grad_gain_first,
            grad_shift_first,
            grad_weight_in,
            grad_bias_in,
            grad_weight_down,
            grad_bias_down,
            grad_gain_second,
            grad_shift_second,
        ),
        devices,
    )
    owned = (
        lax.psum_scatter(all_flat[0], "dp", scatter_dimension=0, tiled=True),
        lax.psum_scatter(all_flat[1], "dp", scatter_dimension=0, tiled=True),
        lax.psum_scatter(all_flat[2], "dp", scatter_dimension=0, tiled=True),
        lax.psum_scatter(all_flat[3], "dp", scatter_dimension=0, tiled=True),
        lax.psum_scatter(all_flat[4], "dp", scatter_dimension=0, tiled=True),
        lax.psum_scatter(all_flat[5], "dp", scatter_dimension=0, tiled=True),
        lax.psum_scatter(all_flat[6], "dp", scatter_dimension=0, tiled=True),
        lax.psum_scatter(all_flat[7], "dp", scatter_dimension=0, tiled=True),
        lax.psum_scatter(all_flat[8], "dp", scatter_dimension=0, tiled=True),
        lax.psum_scatter(all_flat[9], "dp", scatter_dimension=0, tiled=True),
        lax.psum_scatter(all_flat[10], "dp", scatter_dimension=0, tiled=True),
        lax.psum_scatter(all_flat[11], "dp", scatter_dimension=0, tiled=True),
        lax.psum_scatter(all_flat[12], "dp", scatter_dimension=0, tiled=True),
    )
    shaped = tuple((piece.reshape(shape) for piece, shape in zip(owned, shard_shapes)))
    return (
        to_low(encoded),
        grad_tokens,
        shaped[0],
        shaped[1],
        shaped[2],
        shaped[3],
        shaped[4],
        shaped[5],
        shaped[6],
        shaped[7],
        shaped[8],
        shaped[9],
        shaped[10],
        shaped[11],
        shaped[12],
    )


def solution(mesh):
    in_specs = (
        P("dp", None),
        P("dp"),
        P("dp", None),
        P("dp"),
        P("dp"),
        P("dp", None),
        P("dp"),
        P("dp"),
        P("dp"),
        P("dp", None),
        P("dp"),
        P("dp", None),
        P("dp"),
        P("dp"),
        P("dp"),
        P("dp", None),
    )
    out_specs = (
        P("dp", None),
        P("dp", None),
        P("dp", None),
        P("dp"),
        P("dp"),
        P("dp", None),
        P("dp"),
        P("dp"),
        P("dp"),
        P("dp", None),
        P("dp"),
        P("dp", None),
        P("dp"),
        P("dp"),
        P("dp"),
    )
    return jax.shard_map(body, mesh=mesh, in_specs=in_specs, out_specs=out_specs, check_vma=False)
```

profile of v0, /device:TPU:0, one launch (start us, length us, event | category | flops | bytes accessed | tf_op | source)
XLA Modules:
  0.0 775.0 jit_solution(10823627346046776832)
XLA Ops:
  17.6 42.6 %all-reduce.24 = (bf16[3072]{0:T(1024)(128)(2,1)S(1)}, bf16[768]{0:T(1024)(128)(2,1)S(1)}, bf16[768]{0:T(1024)(128)(2,1)S(1)}, bf16[768]{0:T(1024)(128)(2,1)S(1)...) all-reduce(bf16[3072]{0:T(1024)(128)(2,1)S(1)} %dynamic-update-slic, ...), channel_id=1, replica_groups=mesh['dp'=32] {'dp'}, use_global_device_ids=true, to_apply=%add.5 | all-reduce | flops 9216 | bytes 36864
  61.3 12.6 %all-gather.5.cloned.1.call-done = bf16[768,2304]{1,0:T(8,128)(2,1)} async-done(((bf16[24,2304]{1,0:T(8,128)(2,1)}), bf16[768,2304]{1,0:T(8,128)(2,1)}) %all-gather.5.cloned.1.call-update) | async-done | bytes 3538960 | tf_op jit(solution)/shard_map/all_gather | solution.py:93
  73.9 2.8 fusion
  77.7 52.1 %all-gather.7.cloned.1.call-done = bf16[768,768]{1,0:T(8,128)(2,1)} async-done(((bf16[24,768]{1,0:T(8,128)(2,1)}), bf16[768,768]{1,0:T(8,128)(2,1)}) %all-gather.7.cloned.1.call-update) | async-done | bytes 1179664 | tf_op jit(solution)/shard_map/all_gather | solution.py:96
  129.8 1.7 fusion.41
  131.8 63.5 %all-gather.9.cloned.1.call-done = bf16[768,3072]{1,0:T(8,128)(2,1)} async-done(((bf16[24,3072]{1,0:T(8,128)(2,1)}), bf16[768,3072]{1,0:T(8,128)(2,1)}) %all-gather.9.cloned.1.call-update) | async-done | bytes 4718608 | tf_op jit(solution)/shard_map/all_gather | solution.py:102
  195.3 8.4 %multiply_convert_fusion = (bf16[128,3072]{1,0:T(8,128)(2,1)S(1)}, f32[128,3072]{1,0:T(8,128)}, f32[128,3072]{1,0:T(8,128)}) fusion(f32[3072]{0:T(1024)S(1)} %convert_element_type.114, bf16[768,3072]{1,0:T(8,128)(2,1)} %all-gather.9.cloned.1.call-done, f32[128,768]{1,0:T(8,128)S(1)} %get-tuple-element.63, f32[768]{0:T(1024)S(1)} %convert_element_type.112, ...), kind=kOutput, calls=%fused_computation.8 | convolution fusion | flops 630423552 | bytes 9063424 | tf_op jit(solution)/shard_map/dot_general | solution.py:29
  203.7 56.8 %all-gather.11.cloned.1.call-done = bf16[3072,768]{1,0:T(8,128)(2,1)} async-done(((bf16[96,768]{1,0:T(8,128)(2,1)}), bf16[3072,768]{1,0:T(8,128)(2,1)}) %all-gather.11.cloned.1.call-update) | async-done | bytes 4718608 | tf_op jit(solution)/shard_map/all_gather | solution.py:104
  260.6 3.4 fusion.42
  266.6 2.4 convert_reduce_fusion
  269.1 2.4 multiply_reduce_fusion.1
  277.5 5.2 fusion.33
  282.6 5.1 fusion.44
  287.8 1.6 reshape.264
  291.2 3.9 convolution_bitcast_fusion
  295.1 8.0 %copy.57 = f32[768,2304]{1,0:T(8,128)} copy(f32[768,2304]{0,1:T(8,128)} %convolution_bitcast_fusion) | data formatting | bytes 14155776 | tf_op jit(solution)/shard_map/dot_general | solution.py:33
  303.1 6.6 reshape.260
  309.7 8.1 %reshape.272 = f32[32,73728]{1,0:T(8,128)} reshape(f32[768,3072]{1,0:T(8,128)} %fusion.33) | data formatting | bytes 18874368 | tf_op jit(solution)/shard_map/reshape | solution.py:52
  317.9 8.1 %reshape.276 = f32[32,73728]{1,0:T(8,128)} reshape(f32[3072,768]{1,0:T(8,128)} %fusion.44) | data formatting | bytes 18874368 | tf_op jit(solution)/shard_map/reshape | solution.py:52
  339.3 46.1 %all-reduce.22 = (f32[32,24]{1,0:T(8,128)}, f32[32,24]{1,0:T(8,128)}, f32[32,24]{1,0:T(8,128)}, f32[32,24]{1,0:T(8,128)}, f32[32,24]{1,0:T(8,128)}, /*index=5*/f...) all-reduce(f32[32,24]{1,0:T(8,128)} %slice.29, ...), channel_id=3, replica_groups=mesh['dp'=32] {'dp'}, use_global_device_ids=true, to_apply=%region_15.16.clone | all-reduce | flops 9216 | bytes 73728
  391.4 3.2 convolution_add_fusion.3
  394.7 363.6 %all-reduce.27.cloned.1.call-done = (f32[32,55296]{1,0:T(8,128)}, f32[32,18432]{1,0:T(8,128)}, f32[32,73728]{1,0:T(8,128)}, f32[32,73728]{1,0:T(8,128)}) async-done(((f32[32,55296]{1,0:T(8,128)}, f32[32,18432]{1,0:T(8,128)}, f32[32,73728]{1,0:T(8,128)}, f32[32,73728]{1,0:T(8,128)}), (f32[32,55296]{1,0:T(8,128)}, f32[32,18432]{1,0:T(8,128)}, f32[32,73728]{1,0:T(8,128)}, ...) | async-done | bytes 28311568
  758.2 2.1 dynamic-slice_reduce_fusion.2
  762.3 4.0 dynamic-slice_reduce_fusion
  (143 shorter events, 46.5 us)
Async XLA Ops:
  7.2 66.7 %all-gather.5.cloned.1.call-start = ((), (), s32[]{:S(2)}) async-start(), calls=%async_computation | async-start | bytes 3649536 | tf_op jit(solution)/shard_map/all_gather | solution.py:93
  7.9 121.9 %all-gather.7.cloned.1.call-start = ((), (), s32[]{:S(2)}) async-start(), calls=%async_computation.1 | async-start | bytes 1216512 | tf_op jit(solution)/shard_map/all_gather | solution.py:96
  8.7 186.6 %all-gather.9.cloned.1.call-start = ((), (), s32[]{:S(2)}) async-start(), calls=%async_computation.2 | async-start | bytes 4866048 | tf_op jit(solution)/shard_map/all_gather | solution.py:102
  9.4 251.2 %all-gather.11.cloned.1.call-start = ((), (), s32[]{:S(2)}) async-start(), calls=%async_computation.3 | async-start | bytes 4866048 | tf_op jit(solution)/shard_map/all_gather | solution.py:104
  10.0 748.3 %all-reduce.27.cloned.1.call-start = ((), (), s32[]{:S(2)}) async-start(), calls=%async_computation.4 | async-start | bytes 56623104
  77.0 52.9 %copy-start.8 = (bf16[128,768]{1,0:T(8,128)(2,1)S(1)}, bf16[128,768]{1,0:T(8,128)(2,1)}, u32[]{:S(2)}) copy-start(bf16[128,768]{1,0:T(8,128)(2,1)} %param.16) | copy-start | bytes 589828
  77.7 54.1 %copy-start.10 = (bf16[12,64,128]{2,1,0:T(8,128)(2,1)}, bf16[12,64,128]{2,1,0:T(8,128)(2,1)S(1)}, u32[]{:S(2)}) copy-start(bf16[12,64,128]{2,1,0:T(8,128)(2,1)S(1)} %convolution_convert_fusion.1) | copy-start | bytes 589828
  203.7 60.2 %copy-start.3 = (bf16[128,3072]{1,0:T(8,128)(2,1)}, bf16[128,3072]{1,0:T(8,128)(2,1)S(1)}, u32[]{:S(2)}) copy-start(bf16[128,3072]{1,0:T(8,128)(2,1)S(1)} %get-tuple-element.55) | copy-start | bytes 2359300
  260.6 6.0 slice-start
  260.6 3.6 copy-start.15
  260.6 6.0 slice-start.1
  260.6 6.0 copy-start.20
  263.9 2.6 copy-start.19
  265.9 3.2 slice-start.2
  266.6 2.5 copy-start.16
  266.6 2.5 slice-start.3
  269.0 2.4 copy-start.6
  271.5 1.7 copy-start.2
  271.7 1.4 copy-start.18
  277.5 5.2 copy-start.4
  277.5 5.2 copy-start.17
  287.8 1.6 copy-start.14
  287.8 3.4 copy-start.9
  326.0 65.5 %copy-start = (bf16[768,2304]{1,0:T(8,128)(2,1)S(1)}, bf16[768,2304]{1,0:T(8,128)(2,1)}, u32[]{:S(2)}) copy-start(bf16[768,2304]{1,0:T(8,128)(2,1)} %all-gather.5.cloned.1.call-done) | copy-start | bytes 10616836
  (6 other events, 5.4 us)
Sparse Core Ops, SparseCore 0:
  10.9 62.9 all-gather.4
  76.8 52.9 all-gather.6
  132.7 62.5 all-gather.8
  198.1 62.4 all-gather.10
  326.1 432.0 all-reduce.26
where the time goes:
time: 776 us; the launch traced here: 775 us
  waiting for transfers between devices  551 us (71%)
  blocking collectives  88.7 us (11%)
  local copies, waits for them, and re-layouts  72.5 us (9%)
  matrix products  42.1 us (5%)
  between operations  14.2 us (2%)
    unnamed x6, waiting for transfers between devices  366 us
    unnamed x2, blocking collectives  88.7 us
    all_gather x1, waiting for transfers between devices, body(): lax.all_gather(ff_in_weight, 'dp', axis=0, tiled=True)  63.5 us
    all_gather x1, waiting for transfers between devices, body(): lax.all_gather(ff_out_weight, 'dp', axis=0, tiled=True)  56.8 us
    all_gather x1, waiting for transfers between devices, body(): lax.all_gather(out_weight, 'dp', axis=0, tiled=True)  52.1 us
    reshape x11, local copies, waits for them, and re-layouts, by_owner(): return tuple((g.reshape(devices, -1) for g in gradients))  33.6 us
    unnamed x71, local copies, waits for them, and re-layouts  17.4 us
    dot_general x4, matrix products, matmul(): return jnp.dot(left, right, preferred_element_type=jnp.float32)  16.2 us
  transfers between devices with their start and end apart: 5, of which 5 were waited for; matrix products, arithmetic and copies ran while one was open for 6% of the time, Pallas kernels for 0%

commit v1 on v0

v1 whole, which is shorter than its diff:
```python
import functools

import jax
import jax.numpy as jnp
from jax import lax
from jax.experimental import pallas as pl
from jax.experimental.pallas import tpu as pltpu
from jax.sharding import PartitionSpec as P

HEAD_DIM = 64
SMALL_ROWS = 16
LANES = 128
VMEM_BYTES = 56 * 1024 * 1024
MESH = pl.DeviceIdType.MESH


class Place:
    def __init__(self, devices, core=None):
        self.chips = devices // 2
        side = max(s for s in range(1, self.chips + 1) if s**3 <= self.chips and self.chips % (s * s) == 0)
        self.side = side
        self.depth = self.chips // (side * side)
        me = lax.axis_index("dp")
        self.chip = me // 2
        self.own_core = lax.rem(me, 2)
        self.core = self.own_core if core is None else core(self.own_core)
        first = self.core == 0
        self.step_a = side * side
        self.step_s = jnp.where(first, side, 1)
        self.step_t = jnp.where(first, 1, side)
        self.pos_a = self.chip // self.step_a
        mid = lax.rem(self.chip // side, side)
        low = lax.rem(self.chip, side)
        self.pos_s = jnp.where(first, mid, low)
        self.pos_t = jnp.where(first, low, mid)

    def at(self, da, ds, dt):
        a = lax.rem(self.pos_a + da, self.depth)
        s = lax.rem(self.pos_s + ds, self.side)
        t = lax.rem(self.pos_t + dt, self.side)
        return a * self.step_a + s * self.step_s + t * self.step_t

    def device(self, da, ds, dt):
        return self.at(da, ds, dt) * 2 + self.own_core

    def sibling(self):
        return self.chip * 2 + 1 - self.own_core

    def peers(self):
        found = [self.sibling()]
        found += [self.device(d, 0, 0) for d in range(1, self.depth)]
        found += [self.device(0, d, 0) for d in range(1, self.side)]
        found += [self.device(0, 0, d) for d in range(1, self.side)]
        return found


def greet(place):
    barrier = pltpu.get_barrier_semaphore()
    peers = place.peers()
    for peer in peers:
        pl.semaphore_signal(barrier, inc=1, device_id=(peer,), device_id_type=MESH)
    pl.semaphore_wait(barrier, len(peers))


def gather_kernel(devices, count, *refs):
    shards, fulls = refs[:count], refs[count : 2 * count]
    (send_a, recv_a, send_s, recv_s, send_t, recv_t, send_c, recv_c, own_sem) = refs[2 * count :]
    place = Place(devices)
    depth, side = place.depth, place.side
    core = place.core
    greet(place)
    started = []

    def send(source, full, chip, ssem, rsem, device):
        copy = pltpu.make_async_remote_copy(
            src_ref=source, dst_ref=full.at[chip, core], send_sem=ssem, recv_sem=rsem,
            device_id=(device,), device_id_type=MESH)
        copy.start()
        started.append(copy)

    def arrived(w, chip, rsem, from_core):
        full = fulls[w]
        pltpu.make_async_remote_copy(
            src_ref=full.at[chip, from_core], dst_ref=full.at[chip, from_core], send_sem=rsem, recv_sem=rsem,
            device_id=(place.sibling(),), device_id_type=MESH).wait_recv()

    def pass_on(w, source, chip, da, ds, dt, to_s, to_t):
        full = fulls[w]
        if to_t:
            for d in range(1, side):
                at = da * side + ds
                send(source, full, chip, send_t.at[w, d - 1, at], recv_t.at[w, d - 1, at], place.device(0, 0, d))
        if to_s:
            for d in range(1, side):
                send(source, full, chip, send_s.at[w, d - 1, da], recv_s.at[w, d - 1, da], place.device(0, d, 0))
        at = (da * side + ds) * side + dt
        send(source, full, chip, send_c.at[w, at], recv_c.at[w, at], place.sibling())

    own = place.at(0, 0, 0)
    own_copies = []
    for w in range(count):
        for d in range(1, depth):
            send(shards[w], fulls[w], own, send_a.at[w, d - 1], recv_a.at[w, d - 1], place.device(d, 0, 0))
        pass_on(w, shards[w], own, 0, 0, 0, True, True)
        local = pltpu.make_async_copy(shards[w], fulls[w].at[own, core], own_sem.at[w])
        local.start()
        own_copies.append(local)
    for da in range(1, depth):
        for w in range(count):
            chip = place.at(depth - da, 0, 0)
            arrived(w, chip, recv_a.at[w, da - 1], core)
            pass_on(w, fulls[w].at[chip, core], chip, da, 0, 0, True, True)
    for da in range(depth):
        for ds in range(1, side):
            for w in range(count):
                chip = place.at((depth - da) % depth, side - ds, 0)
                arrived(w, chip, recv_s.at[w, ds - 1, da], core)
                pass_on(w, fulls[w].at[chip, core], chip, da, ds, 0, False, True)
    for da in range(depth):
        for ds in range(side):
            for dt in range(1, side):
                for w in range(count):
                    chip = place.at((depth - da) % depth, (side - ds) % side, side - dt)
                    arrived(w, chip, recv_t.at[w, dt - 1, da * side + ds], core)
                    pass_on(w, fulls[w].at[chip, core], chip, da, ds, dt, False, False)
    other = Place(devices, lambda own_core: 1 - own_core)
    for da in range(depth):
        for ds in range(side):
            for dt in range(side):
                for w in range(count):
                    chip = other.at((depth - da) % depth, (side - ds) % side, (side - dt) % side)
                    arrived(w, chip, recv_c.at[w, (da * side + ds) * side + dt], 1 - core)
    for copy in started:
        copy.wait_send()
    for local in own_copies:
        local.wait()


def gather_all(shards, devices):
    chips = devices // 2
    side = max(s for s in range(1, chips + 1) if s**3 <= chips and chips % (s * s) == 0)
    depth = chips // (side * side)
    count = len(shards)
    dma = pltpu.SemaphoreType.DMA
    vmem = pl.BlockSpec(memory_space=pltpu.VMEM)
    pairs = [(count, depth - 1), (count, side - 1, depth), (count, side - 1, depth * side), (count, chips)]
    scratch = []
    for shape in pairs:
        scratch += [dma(shape), dma(shape)]
    return pl.pallas_call(
        functools.partial(gather_kernel, devices, count),
        out_shape=[jax.ShapeDtypeStruct((chips, 2) + s.shape, s.dtype) for s in shards],
        in_specs=[vmem] * count,
        out_specs=[vmem] * count,
        scratch_shapes=scratch + [dma((count,))],
        compiler_params=pltpu.CompilerParams(
            collective_id=0, has_side_effects=True, vmem_limit_bytes=VMEM_BYTES),
        cost_estimate=pl.CostEstimate(flops=0, bytes_accessed=16_000_000, transcendentals=0),
        name="gather_parameters",
    )(*shards)


def scatter_kernel(devices, count, *refs):
    parts, outs = refs[:count], refs[count : 2 * count]
    held = refs[2 * count : 3 * count]
    from_t = refs[3 * count : 4 * count]
    from_s = refs[4 * count : 5 * count]
    from_a = refs[5 * count : 6 * count]
    (send_a, recv_a, send_s, recv_s, send_t, recv_t, send_c, recv_c) = refs[6 * count :]
    place = Place(devices)
    other = Place(devices, lambda own_core: 1 - own_core)
    depth, side = place.depth, place.side
    core = place.core
    greet(place)
    started = []

    def send(source, target, ssem, rsem, device):
        copy = pltpu.make_async_remote_copy(
            src_ref=source, dst_ref=target, send_sem=ssem, recv_sem=rsem,
            device_id=(device,), device_id_type=MESH)
        copy.start()
        started.append(copy)

    def arrived(target, rsem):
        pltpu.make_async_remote_copy(
            src_ref=target, dst_ref=target, send_sem=rsem, recv_sem=rsem,
            device_id=(place.sibling(),), device_id_type=MESH).wait_recv()

    order = [(da, ds, dt) for dt in range(1, side) for ds in list(range(1, side)) + [0] for da in list(range(1, depth)) + [0]]
    order += [(da, ds, 0) for ds in range(1, side) for da in list(range(1, depth)) + [0]]
    order += [(da, 0, 0) for da in list(range(1, depth)) + [0]]

    def number(da, ds, dt):
        return (da * side + ds) * side + dt

    for w in range(count):
        for da, ds, dt in order:
            chip = other.at(da, ds, dt)
            at = number(da, ds, dt)
            send(parts[w].at[chip, 1 - core], held[w].at[chip], send_c.at[w, at], recv_c.at[w, at], place.sibling())

    def collect(w, da, ds, dt):
        chip = place.at(da, ds, dt)
        arrived(held[w].at[chip], recv_c.at[w, number(da, ds, dt)])
        total = parts[w][chip, core].astype(jnp.float32) + held[w][chip].astype(jnp.float32)
        if dt == 0:
            for d in range(1, side):
                at = da * side + ds
                arrived(from_t[w].at[d - 1, at], recv_t.at[w, d - 1, at])
                total = total + from_t[w][d - 1, at].astype(jnp.float32)
            if ds == 0:
                for d in range(1, side):
                    arrived(from_s[w].at[d - 1, da], recv_s.at[w, d - 1, da])
                    total = total + from_s[w][d - 1, da].astype(jnp.float32)
                if da == 0:
                    for d in range(1, depth):
                        arrived(from_a[w].at[d - 1], recv_a.at[w, d - 1])
                        total = total + from_a[w][d - 1].astype(jnp.float32)
        return chip, total

    for dt in range(1, side):
        for w in range(count):
            for ds in list(range(1, side)) + [0]:
                for da in list(range(1, depth)) + [0]:
                    chip, total = collect(w, da, ds, dt)
                    held[w][chip] = total.astype(held[w].dtype)
                    at = da * side + ds
                    send(held[w].at[chip], from_t[w].at[dt - 1, at], send_t.at[w, dt - 1, at],
                         recv_t.at[w, dt - 1, at], place.device(0, 0, dt))
    for ds in range(1, side):
        for w in range(count):
            for da in list(range(1, depth)) + [0]:
                chip, total = collect(w, da, ds, 0)
                held[w][chip] = total.astype(held[w].dtype)
                send(held[w].at[chip], from_s[w].at[ds - 1, da], send_s.at[w, ds - 1, da],
                     recv_s.at[w, ds - 1, da], place.device(0, ds, 0))
    for w in range(count):
        for da in range(1, depth):
            chip, total = collect(w, da, 0, 0)
            held[w][chip] = total.astype(held[w].dtype)
            send(held[w].at[chip], from_a[w].at[da - 1], send_a.at[w, da - 1],
                 recv_a.at[w, da - 1], place.device(da, 0, 0))
    for w in range(count):
        outs[w][...] = collect(w, 0, 0, 0)[1]
    for copy in started:
        copy.wait_send()


def scatter_all(parts, devices):
    chips = devices // 2
    side = max(s for s in range(1, chips + 1) if s**3 <= chips and chips % (s * s) == 0)
    depth = chips // (side * side)
    count = len(parts)
    dma = pltpu.SemaphoreType.DMA
    vmem = pl.BlockSpec(memory_space=pltpu.VMEM)
    pairs = [(count, depth - 1), (count, side - 1, depth), (count, side - 1, depth * side), (count, chips)]
    scratch = []
    for lead in ((chips,), (side - 1, depth * side), (side - 1, depth), (depth - 1,)):
        scratch += [pltpu.VMEM(lead + p.shape[2:], p.dtype) for p in parts]
    for shape in pairs:
        scratch += [dma(shape), dma(shape)]
    return pl.pallas_call(
        functools.partial(scatter_kernel, devices, count),
        out_shape=[jax.ShapeDtypeStruct(p.shape[2:], jnp.float32) for p in parts],
        in_specs=[vmem] * count,
        out_specs=[vmem] * count,
        scratch_shapes=scratch,
        compiler_params=pltpu.CompilerParams(
            collective_id=1, has_side_effects=True, vmem_limit_bytes=VMEM_BYTES),
        cost_estimate=pl.CostEstimate(flops=0, bytes_accessed=16_000_000, transcendentals=0),
        name="scatter_gradients",
    )(*parts)


def pack_rows(vectors, blocks, dtype):
    rows = []
    for v in vectors:
        piece = v.astype(dtype).reshape(blocks, 1, -1)
        rows.append(jnp.pad(piece, ((0, 0), (0, 0), (0, LANES - piece.shape[2]))))
    rows.append(jnp.zeros((blocks, SMALL_ROWS - len(vectors), LANES), dtype))
    return jnp.concatenate(rows, axis=1)


def unpack_rows(packed, lengths):
    return [packed[:, j, :n].reshape(-1) for j, n in enumerate(lengths)]


def gather_params(matrices, vectors, devices):
    lengths = [v.shape[0] for v in vectors]
    small = pack_rows(vectors, 1, jnp.bfloat16)[0]
    if devices > 32:
        full = [lax.all_gather(m, "dp", axis=0, tiled=True) for m in matrices]
        small_full = lax.all_gather(small, "dp", axis=0)
        return full, unpack_rows(small_full, lengths)
    *gathered, small_full = gather_all([*matrices, small], devices)
    full = [g.reshape(devices * m.shape[0], m.shape[1]) for g, m in zip(gathered, matrices)]
    return full, unpack_rows(small_full.reshape(devices, SMALL_ROWS, LANES), lengths)


def scatter_grads(matrices, vectors, devices):
    lengths = [v.shape[0] // devices for v in vectors]
    small = pack_rows(vectors, devices, jnp.float32)
    if devices > 32:
        owned = [lax.psum_scatter(m, "dp", scatter_dimension=0, tiled=True) for m in matrices]
        small_owned = lax.psum_scatter(small, "dp", scatter_dimension=0, tiled=True)[0]
    else:
        chips = devices // 2
        low = [to_low(m).reshape(chips, 2, m.shape[0] // devices, m.shape[1]) for m in matrices]
        small = small.reshape(chips, 2, SMALL_ROWS, LANES)
        *owned, small_owned = scatter_all([*low, small], devices)
    return owned, [small_owned[j, :n] for j, n in enumerate(lengths)]


def layer_norm(hidden, gain, shift):
    center = jnp.mean(hidden, axis=-1, keepdims=True)
    centered = hidden - center
    spread = jnp.mean(centered * centered, axis=-1, keepdims=True)
    return centered * lax.rsqrt(spread + 1e-06) * gain + shift


def gelu_exact(values):
    return jax.nn.gelu(values, approximate=False)


def to_low(values):
    return values.astype(jnp.bfloat16)


def as_float(values):
    return values.astype(jnp.float32)


def matmul(left, right):
    return jnp.dot(left, right, preferred_element_type=jnp.float32)


def matmul_left_t(left, right):
    return lax.dot_general(
        left, right, (((0,), (0,)), ((), ())), preferred_element_type=jnp.float32
    )


def matmul_right_t(left, right):
    return lax.dot_general(
        left, right, (((1,), (1,)), ((), ())), preferred_element_type=jnp.float32
    )


def masked_scores(queries, keys, allowed):
    raw = jnp.einsum(
        "hqd,hkd->hqk", queries, keys, preferred_element_type=jnp.float32
    ) * HEAD_DIM ** (-0.5)
    return jnp.where(allowed[None], raw, -1e30)


def body(
    tokens,
    lengths,
    qkv_weight,
    query_bias,
    value_bias,
    out_weight,
    out_bias,
    norm_one_gain,
    norm_one_shift,
    ff_in_weight,
    ff_in_bias,
    ff_out_weight,
    ff_out_bias,
    norm_two_gain,
    norm_two_shift,
    out_grad,
):
    rows, width = tokens.shape
    heads = width // HEAD_DIM
    scale = HEAD_DIM ** (-0.5)
    devices = lax.axis_size("dp")
    (weight_qkv, weight_out, weight_in, weight_down), vectors = gather_params(
        (qkv_weight, out_weight, ff_in_weight, ff_out_weight),
        (
            query_bias,
            value_bias,
            out_bias,
            norm_one_gain,
            norm_one_shift,
            ff_out_bias,
            norm_two_gain,
            norm_two_shift,
            ff_in_bias,
        ),
        devices,
    )
    (bias_query, bias_value, bias_out, gain_first, shift_first, bias_down, gain_second,
     shift_second, bias_in) = vectors
    bounds = jnp.cumsum(lengths)
    position = jnp.arange(rows, dtype=jnp.int32)
    segments = jnp.sum((position[:, None] >= bounds[None, :]).astype(jnp.int32), axis=1)
    allowed = segments[:, None] == segments[None, :]
    zero_keys = jnp.zeros((width,), jnp.float32)
    qkv_bias = jnp.concatenate([as_float(bias_query), zero_keys, as_float(bias_value)])
    projected = to_low(matmul(tokens, weight_qkv) + qkv_bias)
    split = projected.reshape(rows, 3, heads, HEAD_DIM).transpose(1, 2, 0, 3)
    queries, keys, values = (split[0], split[1], split[2])
    scores = masked_scores(queries, keys, allowed)
    peak = jnp.max(scores, axis=-1, keepdims=True)
    log_total = peak + jnp.log(jnp.sum(jnp.exp(scores - peak), axis=-1, keepdims=True))
    attend = jnp.exp(scores - log_total)
    context = jnp.einsum("hqk,hkd->qhd", to_low(attend), values, preferred_element_type=jnp.float32)
    context = to_low(context.reshape(rows, width))
    first_sum = as_float(tokens) + matmul(context, weight_out) + as_float(bias_out)
    first_norm, norm_one_pull = jax.vjp(
        layer_norm, first_sum, as_float(gain_first), as_float(shift_first)
    )
    first_low = to_low(first_norm)
    pre_act = matmul(first_low, weight_in) + as_float(bias_in)
    activated = to_low(gelu_exact(pre_act))
    second_sum = first_norm + matmul(activated, weight_down) + as_float(bias_down)
    encoded, norm_two_pull = jax.vjp(
        layer_norm, second_sum, as_float(gain_second), as_float(shift_second)
    )
    grad_second, grad_gain_second, grad_shift_second = norm_two_pull(as_float(out_grad))
    grad_ff = to_low(grad_second)
    grad_weight_down = matmul_left_t(activated, grad_ff)
    grad_bias_down = jnp.sum(as_float(grad_ff), axis=0)
    grad_act = matmul_right_t(grad_ff, weight_down)
    gelu_pull = jax.vjp(gelu_exact, pre_act)[1]
    grad_pre = to_low(gelu_pull(grad_act)[0])
    grad_weight_in = matmul_left_t(first_low, grad_pre)
    grad_bias_in = jnp.sum(as_float(grad_pre), axis=0)
    grad_first = grad_second + matmul_right_t(grad_pre, weight_in)
    grad_first_sum, grad_gain_first, grad_shift_first = norm_one_pull(grad_first)
    grad_attn = to_low(grad_first_sum)
    grad_weight_out = matmul_left_t(context, grad_attn)
    grad_bias_out = jnp.sum(as_float(grad_attn), axis=0)
    grad_context = to_low(matmul_right_t(grad_attn, weight_out))
    grad_heads = grad_context.reshape(rows, heads, HEAD_DIM).transpose(1, 0, 2)
    again_scores = masked_scores(queries, keys, allowed)
    again_attend = jnp.exp(again_scores - log_total)
    grad_values = jnp.einsum(
        "hqk,hqd->hkd", to_low(again_attend), grad_heads, preferred_element_type=jnp.float32
    )
    grad_attend = jnp.einsum("hqd,hkd->hqk", grad_heads, values, preferred_element_type=jnp.float32)
    row_total = jnp.sum(grad_attend * again_attend, axis=-1, keepdims=True)
    grad_scores = to_low(again_attend * (grad_attend - row_total))
    grad_queries = (
        jnp.einsum("hqk,hkd->hqd", grad_scores, keys, preferred_element_type=jnp.float32) * scale
    )
    grad_keys = (
        jnp.einsum("hqk,hqd->hkd", grad_scores, queries, preferred_element_type=jnp.float32) * scale
    )
    grad_qkv = to_low(
        jnp.stack([grad_queries, grad_keys, grad_values])
        .transpose(2, 0, 1, 3)
        .reshape(rows, 3 * width)
    )
    grad_weight_qkv = matmul_left_t(tokens, grad_qkv)
    grad_columns = jnp.sum(as_float(grad_qkv), axis=0)
    grad_bias_query = grad_columns[:width]
    grad_bias_value = grad_columns[2 * width :]
    grad_tokens = grad_first_sum + matmul_right_t(grad_qkv, weight_qkv)
    (own_down, own_in, own_out, own_qkv), own = scatter_grads(
        (grad_weight_down, grad_weight_in, grad_weight_out, grad_weight_qkv),
        (
            grad_bias_query,
            grad_bias_value,
            grad_bias_out,
            grad_gain_first,
            grad_shift_first,
            grad_bias_down,
            grad_gain_second,
            grad_shift_second,
            grad_bias_in,
        ),
        devices,
    )
    return (
        to_low(encoded),
        grad_tokens,
        own_qkv,
        own[0],
        own[1],
        own_out,
        own[2],
        own[3],
        own[4],
        own_in,
        own[8],
        own_down,
        own[5],
        own[6],
        own[7],
    )


def solution(mesh):
    in_specs = (
        P("dp", None),
        P("dp"),
        P("dp", None),
        P("dp"),
        P("dp"),
        P("dp", None),
        P("dp"),
        P("dp"),
        P("dp"),
        P("dp", None),
        P("dp"),
        P("dp", None),
        P("dp"),
        P("dp"),
        P("dp"),
        P("dp", None),
    )
    out_specs = (
        P("dp", None),
        P("dp", None),
        P("dp", None),
        P("dp"),
        P("dp"),
        P("dp", None),
        P("dp"),
        P("dp"),
        P("dp"),
        P("dp", None),
        P("dp"),
        P("dp", None),
        P("dp"),
        P("dp"),
        P("dp"),
    )
    return jax.shard_map(body, mesh=mesh, in_specs=in_specs, out_specs=out_specs, check_vma=False)
```

time: 776 us -> 290 us (0.37)
  waiting for transfers between devices: 551 us -> 0 us
  Pallas kernels: 0 us -> 207 us
  blocking collectives: 88.7 us -> 0 us
  local copies, waits for them, and re-layouts: 72.5 us -> 29.4 us
  between operations: 14.2 us -> 1.25 us
    unnamed x6 -> x0, waiting for transfers between devices: 366 us -> none
    pallas_call x0 -> x2, Pallas kernels: none -> 207 us  [the longest x1 121 us: scatter_all(): pl.pallas_call(functools.partial(scatter_kernel, devices, count), out_sha...]
    all_gather x4 -> x0, waiting for transfers between devices: 185 us -> none  [the longest x1 63.5 us: body(): lax.all_gather(ff_in_weight, 'dp', axis=0, tiled=True)]
    unnamed x2 -> x0, blocking collectives: 88.7 us -> none
    reshape x20 -> x7, local copies, waits for them, and re-layouts: 42.6 us -> 0.57 us  [pack_rows(): piece = v.astype(dtype).reshape(blocks, 1, -1)]
    dot_general x1 -> x0, local copies, waits for them, and re-layouts: 8.02 us -> none  [matmul_left_t(): lax.dot_general(left, right, (((0,), (0,)), ((), ())), preferred_element_...]
    unnamed x71 -> x82, local copies, waits for them, and re-layouts: 17.4 us -> 9.88 us
  transfers between devices with their start and end apart: 5 -> 0, of which waited for: 5 -> 0; matrix products, arithmetic and copies ran while one was open for 6% -> 0% of each run, Pallas kernels for 0% -> 0%
where the time goes in v1:
time: 290 us; the launch traced here: 289 us
  Pallas kernels  207 us (71%)
  matrix products  41.3 us (14%)
  local copies, waits for them, and re-layouts  29.4 us (10%)
  other arithmetic  10.1 us (3%)
    pallas_call x1, Pallas kernels, scatter_all(): pl.pallas_call(functools.partial(scatter_kernel, devices, count), out_sha...  121 us
    pallas_call x1, Pallas kernels, gather_all(): pl.pallas_call(functools.partial(gather_kernel, devices, count), out_shap...  85.6 us
    dot_general x4, matrix products, matmul(): return jnp.dot(left, right, preferred_element_type=jnp.float32)  15.4 us
    dot_general x4, matrix products, matmul_left_t(): lax.dot_general(left, right, (((0,), (0,)), ((), ())), preferred_element_...  11.6 us
    dot_general x4, matrix products, matmul_right_t(): lax.dot_general(left, right, (((1,), (1,)), ((), ())), preferred_element_...  11.4 us
    unnamed x82, local copies, waits for them, and re-layouts  9.88 us
    pad x18, local copies, waits for them, and re-layouts, pack_rows(): rows.append(jnp.pad(piece, ((0, 0), (0, 0), (0, LANES - piece.shape[2]))))  6.02 us

profile of v1, /device:TPU:0, one launch (start us, length us, event | category | flops | bytes accessed | tf_op | source)
XLA Modules:
  0.0 289.0 jit_solution(17829079963695381248)
XLA Ops:
  7.8 85.6 %gather_parameters.1 = (bf16[16,2,24,2304]{3,2,1,0:T(8,128)(2,1)}, bf16[16,2,24,768]{3,2,1,0:T(8,128)(2,1)}, bf16[16,2,24,3072]{3,2,1,0:T(8,128)(2,1)}, bf16[16,...) custom-call(bf16[24,2304]{1,0:T(8,128)(2,1)} %refs_0_.1, bf16[24,768]{1,0:T(8,128)(2,1)} %refs_1_.1, ...), custom_call_target="tpu_custom_call" | custom-call | bytes 16000000 | tf_op jit(solution)/shard_map/gather_parameters/pallas_call | solution.py:150
  93.4 2.2 fusion.30
  97.6 3.3 %fusion = bf16[2304,128]{1,0:T(8,128)(2,1)S(1)} fusion(bf16[768,2304]{1,0:T(8,128)(2,1)} %bitcast.145, bf16[128,768]{1,0:T(8,128)(2,1)} %param.16, f32[2304]{0:T(1024)S(1)} %pad_maximum_fusion), kind=kOutput, calls=%fused_computation.5 | convolution fusion | flops 453574656 | bytes 4334592 | tf_op jit(solution)/shard_map/dot_general | solution.py:334
  104.1 8.4 %multiply_convert_fusion = (bf16[128,3072]{1,0:T(8,128)(2,1)S(1)}, f32[128,3072]{1,0:T(8,128)}, f32[128,3072]{1,0:T(8,128)}) fusion(f32[3072]{0:T(1024)S(1)} %reshape.345, bf16[768,3072]{1,0:T(8,128)(2,1)} %bitcast.141, f32[128,768]{1,0:T(8,128)S(1)} %get-tuple-element.77, f32[768]{0:T(1024)S(1)} %reshape.344, f32[768]{0:T(1024)S(1)} %reshape.343, ...), kind=kOutput, calls=%fused_computation.10 | convolution fusion | flops 630423552 | bytes 9063424 | tf_op jit(solution)/shard_map/dot_general | solution.py:334
  112.5 3.2 %fusion.34 = (f32[128]{0:T(128)S(1)}, f32[128,768]{1,0:T(8,128)S(1)}) fusion(f32[768]{0:T(1024)S(1)} %copy-done.22, bf16[128,3072]{1,0:T(8,128)(2,1)S(1)} %get-tuple-element.53, bf16[3072,768]{1,0:T(8,128)(2,1)} %bitcast.137, f32[768]{0:T(1024)S(1)} %reshape.344, f32[768]{0:T(1024)S(1)} %reshape.343, f32[128]{0:T(128)S(1)} %fusion.23, ...), kind=kOutput, calls=%fused_computation.111 | convolution fusion | flops 604667776 | bytes 6302208 | tf_op jit(solution)/shard_map/dot_general | solution.py:334
  117.1 1.4 reshape.347
  118.5 1.8 fusion.16
  121.5 1.4 reshape.348
  122.9 2.0 fusion.28
  125.6 5.7 %convert_reduce_fusion = (f32[3072]{0:T(1024)}, bf16[128,3072]{1,0:T(8,128)(2,1)S(1)}) fusion(f32[128,3072]{1,0:T(8,128)} %get-tuple-element.54, f32[128,3072]{1,0:T(8,128)} %get-tuple-element.78, bf16[128,768]{1,0:T(8,128)(2,1)S(1)} %get-tuple-element.44, bf16[3072,768]{1,0:T(8,128)(2,1)} %bitcast.138), kind=kOutput, calls=%fused_computation.8 | convolution fusion | flops 610268160 | bytes 8859648 | tf_op jit(solution)/shard_map/dot_general | solution.py:344
  131.4 2.4 multiply_reduce_fusion.1
  138.6 1.3 multiply_reduce_fusion
  142.0 2.1 convolution_add_fusion.3
  144.1 3.5 %convolution_convert_fusion.2 = bf16[3072,768]{1,0:T(8,128)(2,1)} fusion(bf16[128,3072]{1,0:T(8,128)(2,1)S(1)} %get-tuple-element.53, bf16[128,768]{1,0:T(8,128)(2,1)S(1)} %copy-done.13), kind=kOutput, calls=%fused_computation.2 | convolution fusion | flops 606339072 | bytes 5701632 | tf_op jit(solution)/shard_map/dot_general | solution.py:338
  147.6 3.7 %convolution_convert_fusion.1 = bf16[768,3072]{1,0:T(8,128)(2,1)} fusion(bf16[128,3072]{1,0:T(8,128)(2,1)S(1)} %copy-done.3, f32[128,768]{1,0:T(8,128)S(1)} %get-tuple-element.77, f32[768]{0:T(1024)S(1)} %reshape.344, f32[768]{0:T(1024)S(1)} %reshape.343, f32[128]{0:T(128)S(1)} %copy-done.28, f32[128]{0:T(128)S(1)} %copy-done.18), kind=kOutput, calls=%fused_computation.1 | convolution fusion | flops 606830592 | bytes 5905408 | tf_op jit(solution)/shard_map/dot_general | solution.py:338
  151.3 1.5 convolution_convert_fusion.3
  152.9 2.9 %convolution_convert_fusion = bf16[2304,768]{0,1:T(8,128)(2,1)} fusion(bf16[128,2304]{0,1:T(8,128)(2,1)S(1)} %bitcast.135, bf16[128,768]{1,0:T(8,128)(2,1)S(1)} %copy-done.11), kind=kOutput, calls=%fused_computation | convolution fusion | flops 454754304 | bytes 4325376 | tf_op jit(solution)/shard_map/dot_general | solution.py:338
  156.8 1.5 concatenate.11
  158.3 121.4 %scatter_gradients.1 = (f32[96,768]{1,0:T(8,128)}, f32[24,3072]{1,0:T(8,128)}, f32[24,768]{1,0:T(8,128)}, f32[24,2304]{1,0:T(8,128)}, f32[16,128]{1,0:T(8,128)}) custom-call(bf16[16,2,96,768]{3,2,1,0:T(8,128)(2,1)} %bitcast.131, bf16[16,2,24,3072]{3,2,1,0:T(8,128)(2,1)} %bitcast.132, bf16[16,2,24,768]{3,2,1,0:T(8,128)(2,1)} %bitcast.136, ...), custom_call_target="tpu_custom_call" | custom-call | bytes 16000000 | tf_op jit(solution)/shard_map/scatter_gradients/pallas_call | solution.py:262
  279.7 1.5 slice_bitcast_fusion.9
  282.4 1.6 copy.102
  284.0 1.5 copy.103
  285.6 1.7 copy.104
  287.3 1.7 copy.105
  (153 shorter events, 24.3 us)
Async XLA Ops:
  97.6 3.4 %copy-start.36 = (s32[2]{0:T(128)S(1)}, s32[2]{0:T(128)}, u32[]{:S(2)}) copy-start(s32[2]{0:T(128)} %param.17) | copy-start | bytes 28
  103.4 9.1 %copy-start.16 = (f32[128]{0:T(128)}, f32[128]{0:T(128)S(1)}, u32[]{:S(2)}) copy-start(f32[128]{0:T(128)S(1)} %broadcast_multiply_fusion.1) | copy-start | bytes 1540
  104.1 8.4 %copy-start.26 = (f32[128]{0:T(128)}, f32[128]{0:T(128)S(1)}, u32[]{:S(2)}) copy-start(f32[128]{0:T(128)S(1)} %fusion.23) | copy-start | bytes 1540
  104.1 8.4 %copy-start.22 = (f32[768]{0:T(1024)S(1)}, f32[768]{0:T(1024)}, u32[]{:S(2)}) copy-start(f32[768]{0:T(1024)} %reshape.346) | copy-start | bytes 9220
  112.5 4.0 %copy-start.14 = (bf16[32,1,24]{2,1,0:T(2,128)(2,1)S(1)}, bf16[32,1,24]{2,1,0:T(2,128)(2,1)}, u32[]{:S(2)}) copy-start(bf16[32,1,24]{2,1,0:T(2,128)(2,1)} %get-tuple-element.56) | copy-start | bytes 4612
  112.5 4.0 %copy-start.15 = (bf16[32,1,24]{2,1,0:T(2,128)(2,1)S(1)}, bf16[32,1,24]{2,1,0:T(2,128)(2,1)}, u32[]{:S(2)}) copy-start(bf16[32,1,24]{2,1,0:T(2,128)(2,1)} %get-tuple-element.63) | copy-start | bytes 4612
  122.9 8.5 %slice-start = ((s8[4718592]{0:T(1024)(128)(4,1)}), s8[4194304]{0:T(1024)(128)(4,1)S(1)}, s32[]{:S(2)}) async-start(s8[4718592]{0:T(1024)(128)(4,1)} %bitcast.142), calls=%async_computation | async-start | bytes 8388608
  125.6 5.7 %copy-start.12 = (bf16[128,768]{1,0:T(8,128)(2,1)}, bf16[128,768]{1,0:T(8,128)(2,1)S(1)}, u32[]{:S(2)}) copy-start(bf16[128,768]{1,0:T(8,128)(2,1)S(1)} %get-tuple-element.44) | copy-start | bytes 589828
  125.6 5.7 %slice-start.1 = ((s8[4718592]{0:T(1024)(128)(4,1)}), s8[524288]{0:T(1024)(128)(4,1)S(1)}, s32[]{:S(2)}) async-start(s8[4718592]{0:T(1024)(128)(4,1)} %bitcast.142), calls=%async_computation.1 | async-start | bytes 1048576
  125.6 5.7 %copy-start.17 = (f32[128]{0:T(128)S(1)}, f32[128]{0:T(128)}, u32[]{:S(2)}) copy-start(f32[128]{0:T(128)} %copy-done.16) | copy-start | bytes 1540
  125.6 5.7 %copy-start.27 = (f32[128]{0:T(128)S(1)}, f32[128]{0:T(128)}, u32[]{:S(2)}) copy-start(f32[128]{0:T(128)} %copy-done.26) | copy-start | bytes 1540
  131.3 2.4 copy-start.2
  144.1 3.6 %copy-start.3 = (bf16[128,3072]{1,0:T(8,128)(2,1)S(1)}, bf16[128,3072]{1,0:T(8,128)(2,1)}, u32[]{:S(2)}) copy-start(bf16[128,3072]{1,0:T(8,128)(2,1)} %copy-done.2) | copy-start | bytes 2359300
  144.1 3.6 %copy-start.18 = (f32[128]{0:T(128)S(1)}, f32[128]{0:T(128)}, u32[]{:S(2)}) copy-start(f32[128]{0:T(128)} %copy-done.16) | copy-start | bytes 1540
  144.1 3.6 %copy-start.28 = (f32[128]{0:T(128)S(1)}, f32[128]{0:T(128)}, u32[]{:S(2)}) copy-start(f32[128]{0:T(128)} %copy-done.26) | copy-start | bytes 1540
  147.6 3.7 %copy-start.5 = (bf16[12,64,128]{2,1,0:T(8,128)(2,1)S(1)}, bf16[12,64,128]{2,1,0:T(8,128)(2,1)}, u32[]{:S(2)}) copy-start(bf16[12,64,128]{2,1,0:T(8,128)(2,1)} %copy-done.4) | copy-start | bytes 589828
  147.6 3.7 %copy-start.7 = (bf16[128,768]{1,0:T(8,128)(2,1)S(1)}, bf16[128,768]{1,0:T(8,128)(2,1)}, u32[]{:S(2)}) copy-start(bf16[128,768]{1,0:T(8,128)(2,1)} %copy-done.6) | copy-start | bytes 589828
  152.8 3.1 %copy-start.23 = (f32[768]{0:T(1024)S(1)}, f32[768]{0:T(1024)}, u32[]{:S(2)}) copy-start(f32[768]{0:T(1024)} %get-tuple-element.45) | copy-start | bytes 9220
  152.8 3.2 %copy-start.25 = (f32[768]{0:T(1024)S(1)}, f32[768]{0:T(1024)}, u32[]{:S(2)}) copy-start(f32[768]{0:T(1024)} %get-tuple-element.35) | copy-start | bytes 9220
  152.8 3.3 %copy-start.24 = (f32[768]{0:T(1024)S(1)}, f32[768]{0:T(1024)}, u32[]{:S(2)}) copy-start(f32[768]{0:T(1024)} %get-tuple-element.39) | copy-start | bytes 9220
  152.9 3.5 %copy-start.21 = (f32[768]{0:T(1024)S(1)}, f32[768]{0:T(1024)}, u32[]{:S(2)}) copy-start(f32[768]{0:T(1024)} %get-tuple-element.43) | copy-start | bytes 9220
  152.9 3.6 %copy-start.20 = (f32[768]{0:T(1024)S(1)}, f32[768]{0:T(1024)}, u32[]{:S(2)}) copy-start(f32[768]{0:T(1024)} %get-tuple-element.37) | copy-start | bytes 9220
  152.9 3.7 %copy-start.19 = (f32[768]{0:T(1024)S(1)}, f32[768]{0:T(1024)}, u32[]{:S(2)}) copy-start(f32[768]{0:T(1024)} %get-tuple-element.40) | copy-start | bytes 9220
  152.9 3.7 %copy-start.29 = (f32[3072]{0:T(1024)S(1)}, f32[3072]{0:T(1024)}, u32[]{:S(2)}) copy-start(f32[3072]{0:T(1024)} %get-tuple-element.41) | copy-start | bytes 36868
  (15 other events, 20.3 us)

commit v2 on v1

--- a/solution.py
+++ b/solution.py
@@ -1,4 +1,4 @@
-import functools
+from types import SimpleNamespace
 
 import jax
 import jax.numpy as jnp
@@ -10,7 +10,7 @@
 HEAD_DIM = 64
 SMALL_ROWS = 16
 LANES = 128
-VMEM_BYTES = 56 * 1024 * 1024
+VMEM_BYTES = 60 * 1024 * 1024
 MESH = pl.DeviceIdType.MESH
 
 
@@ -62,116 +62,82 @@
     pl.semaphore_wait(barrier, len(peers))
 
 
-def gather_kernel(devices, count, *refs):
-    shards, fulls = refs[:count], refs[count : 2 * count]
-    (send_a, recv_a, send_s, recv_s, send_t, recv_t, send_c, recv_c, own_sem) = refs[2 * count :]
-    place = Place(devices)
-    depth, side = place.depth, place.side
-    core = place.core
-    greet(place)
-    started = []
-
-    def send(source, full, chip, ssem, rsem, device):
-        copy = pltpu.make_async_remote_copy(
-            src_ref=source, dst_ref=full.at[chip, core], send_sem=ssem, recv_sem=rsem,
-            device_id=(device,), device_id_type=MESH)
-        copy.start()
-        started.append(copy)
-
-    def arrived(w, chip, rsem, from_core):
-        full = fulls[w]
-        pltpu.make_async_remote_copy(
-            src_ref=full.at[chip, from_core], dst_ref=full.at[chip, from_core], send_sem=rsem, recv_sem=rsem,
-            device_id=(place.sibling(),), device_id_type=MESH).wait_recv()
-
-    def pass_on(w, source, chip, da, ds, dt, to_s, to_t):
-        full = fulls[w]
-        if to_t:
-            for d in range(1, side):
-                at = da * side + ds
-                send(source, full, chip, send_t.at[w, d - 1, at], recv_t.at[w, d - 1, at], place.device(0, 0, d))
-        if to_s:
-            for d in range(1, side):
-                send(source, full, chip, send_s.at[w, d - 1, da], recv_s.at[w, d - 1, da], place.device(0, d, 0))
-        at = (da * side + ds) * side + dt
-        send(source, full, chip, send_c.at[w, at], recv_c.at[w, at], place.sibling())
-
-    own = place.at(0, 0, 0)
-    own_copies = []
-    for w in range(count):
-        for d in range(1, depth):
-            send(shards[w], fulls[w], own, send_a.at[w, d - 1], recv_a.at[w, d - 1], place.device(d, 0, 0))
-        pass_on(w, shards[w], own, 0, 0, 0, True, True)
-        local = pltpu.make_async_copy(shards[w], fulls[w].at[own, core], own_sem.at[w])
-        local.start()
-        own_copies.append(local)
-    for da in range(1, depth):
-        for w in range(count):
-            chip = place.at(depth - da, 0, 0)
-            arrived(w, chip, recv_a.at[w, da - 1], core)
-            pass_on(w, fulls[w].at[chip, core], chip, da, 0, 0, True, True)
-    for da in range(depth):
-        for ds in range(1, side):
-            for w in range(count):
-                chip = place.at((depth - da) % depth, side - ds, 0)
-                arrived(w, chip, recv_s.at[w, ds - 1, da], core)
-                pass_on(w, fulls[w].at[chip, core], chip, da, ds, 0, False, True)
-    for da in range(depth):
-        for ds in range(side):
-            for dt in range(1, side):
-                for w in range(count):
-                    chip = place.at((depth - da) % depth, (side - ds) % side, side - dt)
-                    arrived(w, chip, recv_t.at[w, dt - 1, da * side + ds], core)
-                    pass_on(w, fulls[w].at[chip, core], chip, da, ds, dt, False, False)
-    other = Place(devices, lambda own_core: 1 - own_core)
-    for da in range(depth):
-        for ds in range(side):
-            for dt in range(side):
-                for w in range(count):
-                    chip = other.at((depth - da) % depth, (side - ds) % side, (side - dt) % side)
-                    arrived(w, chip, recv_c.at[w, (da * side + ds) * side + dt], 1 - core)
-    for copy in started:
-        copy.wait_send()
-    for local in own_copies:
-        local.wait()
-
-
-def gather_all(shards, devices):
-    chips = devices // 2
-    side = max(s for s in range(1, chips + 1) if s**3 <= chips and chips % (s * s) == 0)
-    depth = chips // (side * side)
-    count = len(shards)
-    dma = pltpu.SemaphoreType.DMA
-    vmem = pl.BlockSpec(memory_space=pltpu.VMEM)
-    pairs = [(count, depth - 1), (count, side - 1, depth), (count, side - 1, depth * side), (count, chips)]
-    scratch = []
-    for shape in pairs:
-        scratch += [dma(shape), dma(shape)]
-    return pl.pallas_call(
-        functools.partial(gather_kernel, devices, count),
-        out_shape=[jax.ShapeDtypeStruct((chips, 2) + s.shape, s.dtype) for s in shards],
-        in_specs=[vmem] * count,
-        out_specs=[vmem] * count,
-        scratch_shapes=scratch + [dma((count,))],
-        compiler_params=pltpu.CompilerParams(
-            collective_id=0, has_side_effects=True, vmem_limit_bytes=VMEM_BYTES),
-        cost_estimate=pl.CostEstimate(flops=0, bytes_accessed=16_000_000, transcendentals=0),
-        name="gather_parameters",
-    )(*shards)
-
-
-def scatter_kernel(devices, count, *refs):
-    parts, outs = refs[:count], refs[count : 2 * count]
-    held = refs[2 * count : 3 * count]
-    from_t = refs[3 * count : 4 * count]
-    from_s = refs[4 * count : 5 * count]
-    from_a = refs[5 * count : 6 * count]
-    (send_a, recv_a, send_s, recv_s, send_t, recv_t, send_c, recv_c) = refs[6 * count :]
+WEIGHTS = 4
+VECTORS = 9
+CHUNK = 384
+
+
+def dot(left, right):
+    return jnp.dot(left, right, preferred_element_type=jnp.float32)
+
+
+def dot_nt(left, right):
+    return lax.dot_general(left, right, (((1,), (1,)), ((), ())), preferred_element_type=jnp.float32)
+
+
+def dot_tn(left, right):
+    return lax.dot_general(left, right, (((0,), (0,)), ((), ())), preferred_element_type=jnp.float32)
+
+
+def erf_rational(x):
+    x = jnp.clip(x, -3.832506856900711, 3.832506856900711)
+    y = x * x
+    top = jnp.full_like(y, 0.00022905065861350646)
+    for c in (0.0034082910107109506, 0.050955695062380861, 0.18520832239976145, 1.128379143519084):
+        top = top * y + c
+    low = jnp.full_like(y, -1.1791602954361697e-7)
+    for c in (0.000023547966471313185, 0.0010179625278914885, 0.014070470171167667,
+              0.11098505178285362, 0.49746925110067538, 1.0):
+        low = low * y + c
+    return x * top / low
+
+
+def norm_parts(hidden):
+    center = jnp.mean(hidden, axis=-1, keepdims=True)
+    centered = hidden - center
+    inverse = lax.rsqrt(jnp.mean(centered * centered, axis=-1, keepdims=True) + 1e-06)
+    return centered * inverse, inverse
+
+
+def norm_back(grad, gain, unit, inverse):
+    scaled = grad * gain
+    mean_one = jnp.mean(scaled, axis=-1, keepdims=True)
+    mean_two = jnp.mean(scaled * unit, axis=-1, keepdims=True)
+    return inverse * (scaled - mean_one - unit * mean_two)
+
+
+def column_sum(values):
+    return jnp.sum(values, axis=0, keepdims=True)
+
+
+def lane_owner(rows, columns, piece):
+    row = lax.broadcasted_iota(jnp.int32, (rows, columns), 0)
+    column = lax.broadcasted_iota(jnp.int32, (rows, columns), 1)
+    return (lax.rem(column, piece) == row).astype(jnp.bfloat16)
+
+
+def owner_mask(devices, repeat, columns, piece):
+    row = lax.broadcasted_iota(jnp.int32, (devices * repeat, columns), 0)
+    column = lax.broadcasted_iota(jnp.int32, (devices * repeat, columns), 1)
+    start = (row // repeat) * piece
+    return jnp.logical_and(column >= start, column < start + piece)
+
+
+def layer_kernel(devices, ref):
     place = Place(devices)
     other = Place(devices, lambda own_core: 1 - own_core)
-    depth, side = place.depth, place.side
-    core = place.core
-    greet(place)
+    depth, side, core = place.depth, place.side, place.core
+    chips = devices // 2
+    sibling = place.sibling()
+    count = WEIGHTS + 1
+    weights = ref.weight
+    grads = ref.grad
+    held = ref.held
+    from_t = ref.from_t
+    from_s = ref.from_s
+    from_a = ref.from_a
+    shards = ref.shard
+    raws = ref.raw
     started = []
 
     def send(source, target, ssem, rsem, device):
@@ -184,7 +150,177 @@
     def arrived(target, rsem):
         pltpu.make_async_remote_copy(
             src_ref=target, dst_ref=target, send_sem=rsem, recv_sem=rsem,
-            device_id=(place.sibling(),), device_id_type=MESH).wait_recv()
+            device_id=(sibling,), device_id_type=MESH).wait_recv()
+
+    def rows_of(w, chip):
+        rows = 2 * shards[w].shape[0]
+        return pl.ds(pl.multiple_of(chip * rows, rows), rows)
+
+    def block(array, w, chip, of_core):
+        if w == WEIGHTS:
+            return array.at[chip, of_core]
+        return array.at[of_core, rows_of(w, chip)]
+
+    own = place.at(0, 0, 0)
+    piece = ref.vector[0].shape[1]
+    wide = ref.vector[8].shape[1]
+    pack = ref.pack
+    pack[...] = jnp.zeros_like(pack)
+    for j in range(VECTORS):
+        v = ref.vector[j]
+        pack[j : j + 1, 0 : v.shape[1]] = v[...].astype(jnp.float32)
+    weights[WEIGHTS][own, core] = pack[...]
+    greet(place)
+    for w in range(WEIGHTS):
+        send(shards[w], raws[w], ref.raw_send.at[w], ref.raw_recv.at[w], sibling)
+
+    def pass_on(w, chip, da, ds, dt, to_s, to_t):
+        part = block(weights[w], w, chip, core)
+        if to_t:
+            for d in range(1, side):
+                at = da * side + ds
+                send(part, part, ref.g_send_t.at[w, d - 1, at], ref.g_recv_t.at[w, d - 1, at], place.device(0, 0, d))
+        if to_s:
+            for d in range(1, side):
+                send(part, part, ref.g_send_s.at[w, d - 1, da], ref.g_recv_s.at[w, d - 1, da], place.device(0, d, 0))
+        if (da, ds, dt) != (0, 0, 0) or w == WEIGHTS:
+            at = (da * side + ds) * side + dt
+            send(part, part, ref.g_send_c.at[w, at], ref.g_recv_c.at[w, at], sibling)
+
+    def gather_own(w):
+        if w < WEIGHTS:
+            arrived(raws[w], ref.raw_recv.at[w])
+            mine = shards[w][...].astype(jnp.float32)
+            theirs = raws[w][...].astype(jnp.float32)
+            both = jnp.concatenate(
+                [jnp.where(core == 0, mine, theirs), jnp.where(core == 0, theirs, mine)], axis=0).astype(jnp.bfloat16)
+            half = both.shape[1] // 2
+            weights[w][0, rows_of(w, own)] = both[:, :half]
+            weights[w][1, rows_of(w, own)] = both[:, half:]
+        part = block(weights[w], w, own, core)
+        for d in range(1, depth):
+            send(part, part, ref.g_send_a.at[w, d - 1], ref.g_recv_a.at[w, d - 1], place.device(d, 0, 0))
+        pass_on(w, own, 0, 0, 0, True, True)
+
+    def gather_a(w):
+        for da in range(1, depth):
+            chip = place.at(depth - da, 0, 0)
+            arrived(block(weights[w], w, chip, core), ref.g_recv_a.at[w, da - 1])
+            pass_on(w, chip, da, 0, 0, True, True)
+
+    def gather_s(w):
+        for da in range(depth):
+            for ds in range(1, side):
+                chip = place.at((depth - da) % depth, side - ds, 0)
+                arrived(block(weights[w], w, chip, core), ref.g_recv_s.at[w, ds - 1, da])
+                pass_on(w, chip, da, ds, 0, False, True)
+
+    def gather_t(w):
+        for da in range(depth):
+            for ds in range(side):
+                for dt in range(1, side):
+                    chip = place.at((depth - da) % depth, (side - ds) % side, side - dt)
+                    arrived(block(weights[w], w, chip, core), ref.g_recv_t.at[w, dt - 1, da * side + ds])
+                    pass_on(w, chip, da, ds, dt, False, False)
+
+    def gather_c(w):
+        for da in range(depth):
+            for ds in range(side):
+                for dt in range(side):
+                    if (da, ds, dt) == (0, 0, 0) and w < WEIGHTS:
+                        continue
+                    chip = other.at((depth - da) % depth, (side - ds) % side, (side - dt) % side)
+                    arrived(block(weights[w], w, chip, 1 - core),
+                            ref.g_recv_c.at[w, (da * side + ds) * side + dt])
+
+    arrivals = (WEIGHTS, 0, 1, 2, 3)
+    for w in arrivals:
+        gather_own(w)
+    for w in arrivals:
+        gather_a(w)
+    for w in arrivals:
+        gather_s(w)
+
+    tokens = ref.tokens
+    rows, width = tokens.shape
+    hidden = weights[2].shape[2] * 2
+    heads = width // HEAD_DIM
+    scale = HEAD_DIM ** (-0.5)
+    qkv, context = ref.qkv, ref.context
+    ref.tokens_t[...] = tokens[...].T
+    position_r = lax.broadcasted_iota(jnp.int32, (rows, rows), 0)
+    position_c = lax.broadcasted_iota(jnp.int32, (rows, rows), 1)
+    segment_r = jnp.zeros((rows, rows), jnp.int32)
+    segment_c = jnp.zeros((rows, rows), jnp.int32)
+    bound = jnp.int32(0)
+    for slot in range(ref.lengths.shape[0]):
+        bound = bound + ref.lengths[slot]
+        segment_r = segment_r + (position_r >= bound).astype(jnp.int32)
+        segment_c = segment_c + (position_c >= bound).astype(jnp.int32)
+    allowed = segment_r == segment_c
+
+    gather_t(WEIGHTS)
+    gather_c(WEIGHTS)
+    packed = weights[WEIGHTS][...].reshape(devices * SMALL_ROWS, LANES)
+    spread = dot(packed.astype(jnp.bfloat16), lane_owner(LANES, width, piece))
+    spread = jnp.where(owner_mask(devices, SMALL_ROWS, width, piece), spread, 0.0)
+    pick = lane_owner(SMALL_ROWS, devices * SMALL_ROWS, SMALL_ROWS)
+    vectors = dot(pick, spread.astype(jnp.bfloat16))
+    ninth = dot(weights[WEIGHTS][...].reshape(devices, SMALL_ROWS, LANES)[:, VECTORS - 1, :].astype(jnp.bfloat16),
+                lane_owner(LANES, hidden, wide))
+    bias_in = column_sum(jnp.where(owner_mask(devices, 1, hidden, wide), ninth, 0.0))
+    bias_query, bias_value, bias_out, gain_first, shift_first, bias_down, gain_second, shift_second = [
+        vectors[j : j + 1] for j in range(8)]
+    qkv_bias = jnp.concatenate([bias_query, jnp.zeros_like(bias_query), bias_value], axis=1)
+
+    gather_t(0)
+    gather_c(0)
+    half = weights[0].shape[2]
+    for h in range(2):
+        for c in range(0, half, CHUNK):
+            at = h * half + c
+            out = dot(tokens[...], weights[0][h, :, c : c + CHUNK]) + qkv_bias[:, at : at + CHUNK]
+            qkv[:, at : at + CHUNK] = out.astype(jnp.bfloat16)
+    for pair in range(heads // 2):
+        found = []
+        for h in (2 * pair, 2 * pair + 1):
+            q, k, v = [qkv[:, i * width + h * HEAD_DIM : i * width + (h + 1) * HEAD_DIM] for i in range(3)]
+            scores = jnp.where(allowed, dot_nt(q, k) * scale, -1e30)
+            weight = jnp.exp(scores - jnp.max(scores, axis=-1, keepdims=True))
+            weight = weight / jnp.sum(weight, axis=-1, keepdims=True)
+            ref.attend[h] = weight
+            found.append(dot(weight.astype(jnp.bfloat16), v))
+        at = pair * 2 * HEAD_DIM
+        context[:, at : at + 2 * HEAD_DIM] = jnp.concatenate(found, axis=1).astype(jnp.bfloat16)
+    ref.context_t[...] = context[...].T
+
+    gather_t(1)
+    gather_t(2)
+    gather_c(1)
+    attn = jnp.concatenate([dot(context[...], weights[1][h]) for h in range(2)], axis=1)
+    unit_one, inverse_one = norm_parts(tokens[...].astype(jnp.float32) + attn + bias_out)
+    ref.unit_one[...] = unit_one
+    first_norm = unit_one * gain_first + shift_first
+    ref.first_norm[...] = first_norm
+    first_low = first_norm.astype(jnp.bfloat16)
+    ref.first_low[...] = first_low
+    ref.first_t[...] = first_low.T
+    gather_t(3)
+    gather_c(2)
+    half = weights[2].shape[2]
+    for h in range(2):
+        for c in range(0, half, CHUNK):
+            at = h * half + c
+            pre = dot(ref.first_low[...], weights[2][h, :, c : c + CHUNK]) + bias_in[:, at : at + CHUNK]
+            gate = 0.5 + 0.5 * erf_rational(pre * (0.5**0.5))
+            act = (pre * gate).astype(jnp.bfloat16)
+            ref.active[:, at : at + CHUNK] = act
+            ref.active_t[at : at + CHUNK, :] = act.T
+            ref.slope[:, at : at + CHUNK] = gate + pre * (0.3989422804014327 * jnp.exp(-0.5 * pre * pre))
+    gather_c(3)
+    down = jnp.concatenate([dot(ref.active[...], weights[3][h]) for h in range(2)], axis=1)
+    unit_two, inverse_two = norm_parts(ref.first_norm[...] + down + bias_down)
+    ref.encoded[...] = (unit_two * gain_second + shift_second).astype(jnp.bfloat16)
 
     order = [(da, ds, dt) for dt in range(1, side) for ds in list(range(1, side)) + [0] for da in list(range(1, depth)) + [0]]
     order += [(da, ds, 0) for ds in range(1, side) for da in list(range(1, depth)) + [0]]
@@ -193,83 +329,285 @@
     def number(da, ds, dt):
         return (da * side + ds) * side + dt
 
-    for w in range(count):
+    def held_of(w, chip):
+        return held[w].at[chip] if w == WEIGHTS else held[w].at[rows_of(w, chip)]
+
+    def scatter_c(w):
         for da, ds, dt in order:
             chip = other.at(da, ds, dt)
             at = number(da, ds, dt)
-            send(parts[w].at[chip, 1 - core], held[w].at[chip], send_c.at[w, at], recv_c.at[w, at], place.sibling())
+            send(block(grads[w], w, chip, 1 - core), held_of(w, chip), ref.s_send_c.at[w, at],
+                 ref.s_recv_c.at[w, at], sibling)
 
     def collect(w, da, ds, dt):
         chip = place.at(da, ds, dt)
-        arrived(held[w].at[chip], recv_c.at[w, number(da, ds, dt)])
-        total = parts[w][chip, core].astype(jnp.float32) + held[w][chip].astype(jnp.float32)
+        arrived(held_of(w, chip), ref.s_recv_c.at[w, number(da, ds, dt)])
+        total = block(grads[w], w, chip, core)[...].astype(jnp.float32) + held_of(w, chip)[...].astype(jnp.float32)
         if dt == 0:
             for d in range(1, side):
                 at = da * side + ds
-                arrived(from_t[w].at[d - 1, at], recv_t.at[w, d - 1, at])
+                arrived(from_t[w].at[d - 1, at], ref.s_recv_t.at[w, d - 1, at])
                 total = total + from_t[w][d - 1, at].astype(jnp.float32)
             if ds == 0:
                 for d in range(1, side):
-                    arrived(from_s[w].at[d - 1, da], recv_s.at[w, d - 1, da])
+                    arrived(from_s[w].at[d - 1, da], ref.s_recv_s.at[w, d - 1, da])
                     total = total + from_s[w][d - 1, da].astype(jnp.float32)
                 if da == 0:
                     for d in range(1, depth):
-                        arrived(from_a[w].at[d - 1], recv_a.at[w, d - 1])
+                        arrived(from_a[w].at[d - 1], ref.s_recv_a.at[w, d - 1])
                         total = total + from_a[w][d - 1].astype(jnp.float32)
         return chip, total
 
-    for dt in range(1, side):
-        for w in range(count):
+    def relay(w, da, ds, dt, target, ssem, rsem, device):
+        chip, total = collect(w, da, ds, dt)
+        slot = held_of(w, chip)
+        slot[...] = total.astype(held[w].dtype)
+        send(slot, target, ssem, rsem, device)
+
+    def scatter_t(w):
+        for dt in range(1, side):
             for ds in list(range(1, side)) + [0]:
                 for da in list(range(1, depth)) + [0]:
-                    chip, total = collect(w, da, ds, dt)
-                    held[w][chip] = total.astype(held[w].dtype)
                     at = da * side + ds
-                    send(held[w].at[chip], from_t[w].at[dt - 1, at], send_t.at[w, dt - 1, at],
-                         recv_t.at[w, dt - 1, at], place.device(0, 0, dt))
-    for ds in range(1, side):
-        for w in range(count):
+                    relay(w, da, ds, dt, from_t[w].at[dt - 1, at], ref.s_send_t.at[w, dt - 1, at],
+                          ref.s_recv_t.at[w, dt - 1, at], place.device(0, 0, dt))
+
+    def scatter_s(w):
+        for ds in range(1, side):
             for da in list(range(1, depth)) + [0]:
-                chip, total = collect(w, da, ds, 0)
-                held[w][chip] = total.astype(held[w].dtype)
-                send(held[w].at[chip], from_s[w].at[ds - 1, da], send_s.at[w, ds - 1, da],
-                     recv_s.at[w, ds - 1, da], place.device(0, ds, 0))
-    for w in range(count):
+                relay(w, da, ds, 0, from_s[w].at[ds - 1, da], ref.s_send_s.at[w, ds - 1, da],
+                      ref.s_recv_s.at[w, ds - 1, da], place.device(0, ds, 0))
+
+    def scatter_a(w):
         for da in range(1, depth):
-            chip, total = collect(w, da, 0, 0)
-            held[w][chip] = total.astype(held[w].dtype)
-            send(held[w].at[chip], from_a[w].at[da - 1], send_a.at[w, da - 1],
-                 recv_a.at[w, da - 1], place.device(da, 0, 0))
-    for w in range(count):
-        outs[w][...] = collect(w, 0, 0, 0)[1]
+            relay(w, da, 0, 0, from_a[w].at[da - 1], ref.s_send_a.at[w, da - 1],
+                  ref.s_recv_a.at[w, da - 1], place.device(da, 0, 0))
+
+    def finish(w):
+        total = collect(w, 0, 0, 0)[1]
+        if w == WEIGHTS:
+            for j in range(VECTORS):
+                out = ref.own_vector[j]
+                out[...] = total[j : j + 1, : out.shape[1]]
+            return
+        mid = total.shape[0] // 2
+        ref.final[w][...] = jnp.where(core == 0, total[:mid], total[mid:])
+        ref.leave[w][...] = jnp.where(core == 0, total[mid:], total[:mid])
+        send(ref.leave[w], ref.enter[w], ref.f_send.at[w], ref.f_recv.at[w], sibling)
+
+    def put_out(w):
+        arrived(ref.enter[w], ref.f_recv.at[w])
+        mine, theirs = ref.final[w][...], ref.enter[w][...]
+        half = mine.shape[1]
+        ref.own[w][:, :half] = jnp.where(core == 0, mine, theirs)
+        ref.own[w][:, half:] = jnp.where(core == 0, theirs, mine)
+
+    out_grad = ref.out_grad[...].astype(jnp.float32)
+    grad_second = norm_back(out_grad, gain_second, unit_two, inverse_two)
+    grad_ff = grad_second.astype(jnp.bfloat16)
+    ref.grad_ff[...] = grad_ff
+    half = weights[3].shape[2]
+    for h in range(2):
+        for c in range(0, hidden, CHUNK):
+            part = dot(ref.active_t[c : c + CHUNK, :], ref.grad_ff[:, h * half : (h + 1) * half])
+            grads[3][h, c : c + CHUNK, :] = part.astype(jnp.bfloat16)
+    scatter_c(3)
+    grad_gain_second = column_sum(out_grad * unit_two)
+    grad_shift_second = column_sum(out_grad)
+    grad_bias_down = column_sum(grad_ff.astype(jnp.float32))
+    ref.grad_second[...] = grad_second
+    half_in = weights[2].shape[2]
+    bias_parts = []
+    for c in range(0, hidden, CHUNK):
+        back = dot_nt(ref.grad_ff[:, :half], weights[3][0, c : c + CHUNK, :])
+        back = back + dot_nt(ref.grad_ff[:, half:], weights[3][1, c : c + CHUNK, :])
+        part = (back * ref.slope[:, c : c + CHUNK]).astype(jnp.bfloat16)
+        ref.grad_pre[:, c : c + CHUNK] = part
+        bias_parts.append(column_sum(part.astype(jnp.float32)))
+    scatter_t(3)
+    for h in range(2):
+        for c in range(0, half_in, CHUNK):
+            at = h * half_in + c
+            grads[2][h, :, c : c + CHUNK] = dot(ref.first_t[...], ref.grad_pre[:, at : at + CHUNK]).astype(jnp.bfloat16)
+    scatter_c(2)
+    grad_first = ref.grad_second[...] + dot_nt(ref.grad_pre[:, :half_in], weights[2][0])
+    grad_first = grad_first + dot_nt(ref.grad_pre[:, half_in:], weights[2][1])
+    unit_one = ref.unit_one[...]
+    grad_first_sum = norm_back(grad_first, gain_first, unit_one, inverse_one)
+    ref.grad_first_sum[...] = grad_first_sum
+    grad_gain_first = column_sum(grad_first * unit_one)
+    grad_shift_first = column_sum(grad_first)
+    grad_attn = grad_first_sum.astype(jnp.bfloat16)
+    ref.grad_attn[...] = grad_attn
+    grad_bias_out = column_sum(grad_attn.astype(jnp.float32))
+    scatter_t(2)
+    half = weights[1].shape[2]
+    for h in range(2):
+        grads[1][h] = dot(ref.context_t[...], ref.grad_attn[:, h * half : (h + 1) * half]).astype(jnp.bfloat16)
+    scatter_c(1)
+    scatter_s(3)
+    back = dot_nt(ref.grad_attn[:, :half], weights[1][0]) + dot_nt(ref.grad_attn[:, half:], weights[1][1])
+    ref.grad_context[...] = back.astype(jnp.bfloat16)
+    for pair in range(heads // 2):
+        found = [[], [], []]
+        for h in (2 * pair, 2 * pair + 1):
+            q, k, v = [qkv[:, i * width + h * HEAD_DIM : i * width + (h + 1) * HEAD_DIM] for i in range(3)]
+            grad = ref.grad_context[:, h * HEAD_DIM : (h + 1) * HEAD_DIM]
+            weight = ref.attend[h]
+            grad_weight = dot_nt(grad, v)
+            total = jnp.sum(grad_weight * weight, axis=-1, keepdims=True)
+            grad_scores = (weight * (grad_weight - total)).astype(jnp.bfloat16)
+            found[0].append(dot(grad_scores, k) * scale)
+            found[1].append(dot_tn(grad_scores, q) * scale)
+            found[2].append(dot_tn(weight.astype(jnp.bfloat16), grad))
+        for i in range(3):
+            at = i * width + pair * 2 * HEAD_DIM
+            ref.grad_qkv[:, at : at + 2 * HEAD_DIM] = jnp.concatenate(found[i], axis=1).astype(jnp.bfloat16)
+    scatter_t(1)
+    half = weights[0].shape[2]
+    for h in range(2):
+        for c in range(0, half, CHUNK):
+            at = h * half + c
+            grads[0][h, :, c : c + CHUNK] = dot(ref.tokens_t[...], ref.grad_qkv[:, at : at + CHUNK]).astype(jnp.bfloat16)
+    scatter_c(0)
+    columns = column_sum(ref.grad_qkv[...].astype(jnp.float32))
+    found = [columns[:, :width], columns[:, 2 * width :], grad_bias_out, grad_gain_first, grad_shift_first,
+             grad_bias_down, grad_gain_second, grad_shift_second]
+    found = jnp.concatenate(found + [jnp.zeros_like(grad_bias_out)] * (SMALL_ROWS - len(found)), axis=0)
+    mask = owner_mask(devices, SMALL_ROWS, width, piece)
+    spread = jnp.where(mask, jnp.concatenate([found] * devices, axis=0), 0.0)
+    ninth = jnp.where(owner_mask(devices, 1, hidden, wide), jnp.concatenate(bias_parts, axis=1), 0.0)
+    small = jnp.zeros((devices * SMALL_ROWS, LANES), jnp.float32)
+    small_in = jnp.zeros((devices, LANES), jnp.float32)
+    for _ in range(3):
+        low = spread.astype(jnp.bfloat16)
+        small = small + dot_nt(low, lane_owner(LANES, width, piece))
+        spread = spread - low.astype(jnp.float32)
+        low = ninth.astype(jnp.bfloat16)
+        small_in = small_in + dot_nt(low, lane_owner(LANES, hidden, wide))
+        ninth = ninth - low.astype(jnp.float32)
+    row = lax.broadcasted_iota(jnp.int32, (devices, SMALL_ROWS, LANES), 1)
+    small = jnp.where(row == VECTORS - 1, small_in.reshape(devices, 1, LANES), small.reshape(devices, SMALL_ROWS, LANES))
+    grads[WEIGHTS][...] = small.reshape(chips, 2, SMALL_ROWS, LANES)
+    scatter_c(WEIGHTS)
+    scatter_s(2)
+    scatter_t(0)
+    scatter_t(WEIGHTS)
+    half = weights[0].shape[2]
+    grad_tokens = ref.grad_first_sum[...] + dot_nt(ref.grad_qkv[:, :half], weights[0][0])
+    ref.grad_tokens[...] = grad_tokens + dot_nt(ref.grad_qkv[:, half:], weights[0][1])
+    scatter_a(3)
+    scatter_s(1)
+    scatter_a(2)
+    scatter_s(0)
+    scatter_s(WEIGHTS)
+    scatter_a(1)
+    scatter_a(0)
+    scatter_a(WEIGHTS)
+    for w in (3, 2, 1, 0, WEIGHTS):
+        finish(w)
+    for w in (3, 2, 1, 0):
+        put_out(w)
     for copy in started:
         copy.wait_send()
 
 
-def scatter_all(parts, devices):
+def publish_kernel(*refs):
+    for source, target in zip(refs[: len(refs) // 2], refs[len(refs) // 2 :]):
+        target[...] = source[...]
+
+
+def whole_layer(tokens, lengths, matrices, vectors, out_grad, devices):
+    rows, width = tokens.shape
+    hidden = matrices[2].shape[1]
     chips = devices // 2
     side = max(s for s in range(1, chips + 1) if s**3 <= chips and chips % (s * s) == 0)
     depth = chips // (side * side)
-    count = len(parts)
-    dma = pltpu.SemaphoreType.DMA
+    count = WEIGHTS + 1
+
+    def low(*shape):
+        return jax.ShapeDtypeStruct(shape, jnp.bfloat16)
+
+    def full(*shape):
+        return jax.ShapeDtypeStruct(shape, jnp.float32)
+
+    def per_block(*lead):
+        blocks = [low(*lead, 2 * m.shape[0], m.shape[1] // 2) for m in matrices]
+        return blocks + [full(*lead, SMALL_ROWS, LANES)]
+
+    args = dict(
+        tokens=tokens, lengths=lengths, out_grad=out_grad, shard=list(matrices),
+        vector=[v.reshape(1, -1) for v in vectors])
+    outs = dict(
+        encoded=low(rows, width), grad_tokens=full(rows, width),
+        own=[full(*m.shape) for m in matrices],
+        own_vector=[full(1, v.shape[0]) for v in vectors])
+    held = [low(m.shape[0] * devices, m.shape[1] // 2) for m in matrices]
+    halves = [low(2, *h.shape) for h in held]
+    pieces = [full(m.shape[0], m.shape[1] // 2) for m in matrices]
+    small = full(chips, 2, SMALL_ROWS, LANES)
+    heads = width // HEAD_DIM
+    scratch = dict(
+        raw=[low(*m.shape) for m in matrices], weight=halves + [small], grad=halves + [small],
+        held=held + [full(chips, SMALL_ROWS, LANES)],
+        from_t=per_block(side - 1, depth * side), from_s=per_block(side - 1, depth),
+        from_a=per_block(depth - 1), final=pieces, leave=pieces, enter=pieces,
+        pack=full(SMALL_ROWS, LANES),
+        context=low(rows, width), first_low=low(rows, width), grad_ff=low(rows, width),
+        grad_attn=low(rows, width), grad_context=low(rows, width),
+        tokens_t=low(width, rows), context_t=low(width, rows), first_t=low(width, rows),
+        unit_one=full(rows, width), first_norm=full(rows, width),
+        grad_second=full(rows, width), grad_first_sum=full(rows, width),
+        qkv=low(rows, 3 * width), grad_qkv=low(rows, 3 * width),
+        active=low(rows, hidden), grad_pre=low(rows, hidden), active_t=low(hidden, rows),
+        slope=full(rows, hidden), attend=full(heads, rows, rows))
+    by_a, by_s, by_t = (count, depth - 1), (count, side - 1, depth), (count, side - 1, depth * side)
+    by_c, by_w = (count, chips), (WEIGHTS,)
+    sems = dict(
+        g_send_a=by_a, g_recv_a=by_a, s_send_a=by_a, s_recv_a=by_a,
+        g_send_s=by_s, g_recv_s=by_s, s_send_s=by_s, s_recv_s=by_s,
+        g_send_t=by_t, g_recv_t=by_t, s_send_t=by_t, s_recv_t=by_t,
+        g_send_c=by_c, g_recv_c=by_c, s_send_c=by_c, s_recv_c=by_c,
+        raw_send=by_w, raw_recv=by_w, f_send=by_w, f_recv=by_w)
+    sems = {name: pltpu.SemaphoreType.DMA(shape) for name, shape in sems.items()}
     vmem = pl.BlockSpec(memory_space=pltpu.VMEM)
-    pairs = [(count, depth - 1), (count, side - 1, depth), (count, side - 1, depth * side), (count, chips)]
-    scratch = []
-    for lead in ((chips,), (side - 1, depth * side), (side - 1, depth), (depth - 1,)):
-        scratch += [pltpu.VMEM(lead + p.shape[2:], p.dtype) for p in parts]
-    for shape in pairs:
-        scratch += [dma(shape), dma(shape)]
-    return pl.pallas_call(
-        functools.partial(scatter_kernel, devices, count),
-        out_shape=[jax.ShapeDtypeStruct(p.shape[2:], jnp.float32) for p in parts],
-        in_specs=[vmem] * count,
-        out_specs=[vmem] * count,
-        scratch_shapes=scratch,
+    smem = pl.BlockSpec(memory_space=pltpu.SMEM)
+    arg_list, arg_tree = jax.tree.flatten(args)
+    out_list, out_tree = jax.tree.flatten(outs)
+    scratch_list, scratch_tree = jax.tree.flatten(scratch)
+
+    def kernel(*refs):
+        cuts = [len(arg_list), len(arg_list) + len(out_list)]
+        cuts.append(cuts[1] + len(scratch_list))
+        ref = SimpleNamespace(
+            **jax.tree.unflatten(arg_tree, refs[: cuts[0]]),
+            **jax.tree.unflatten(out_tree, refs[cuts[0] : cuts[1]]),
+            **jax.tree.unflatten(scratch_tree, refs[cuts[1] : cuts[2]]),
+            **dict(zip(sems, refs[cuts[2] :])))
+        layer_kernel(devices, ref)
+
+    found = pl.pallas_call(
+        kernel,
+        out_shape=out_list,
+        in_specs=[smem if a is lengths else vmem for a in arg_list],
+        out_specs=[vmem] * len(out_list),
+        scratch_shapes=[pltpu.VMEM(s.shape, s.dtype) for s in scratch_list] + list(sems.values()),
         compiler_params=pltpu.CompilerParams(
-            collective_id=1, has_side_effects=True, vmem_limit_bytes=VMEM_BYTES),
-        cost_estimate=pl.CostEstimate(flops=0, bytes_accessed=16_000_000, transcendentals=0),
-        name="scatter_gradients",
-    )(*parts)
+            collective_id=0, has_side_effects=True, vmem_limit_bytes=VMEM_BYTES),
+        name="encoder_layer",
+    )(*arg_list)
+    found = pl.pallas_call(
+        publish_kernel,
+        out_shape=out_list,
+        in_specs=[vmem] * len(out_list),
+        out_specs=[vmem] * len(out_list),
+        name="publish",
+    )(*found)
+    out = SimpleNamespace(**jax.tree.unflatten(out_tree, found))
+    own_qkv, own_out, own_in, own_down = out.own
+    own = [v.reshape(-1) for v in out.own_vector]
+    return (out.encoded, out.grad_tokens, own_qkv, own[0], own[1], own_out, own[2], own[3], own[4],
+            own_in, own[8], own_down, own[5], own[6], own[7])
 
 
 def pack_rows(vectors, blocks, dtype):
@@ -288,26 +626,16 @@
 def gather_params(matrices, vectors, devices):
     lengths = [v.shape[0] for v in vectors]
     small = pack_rows(vectors, 1, jnp.bfloat16)[0]
-    if devices > 32:
-        full = [lax.all_gather(m, "dp", axis=0, tiled=True) for m in matrices]
-        small_full = lax.all_gather(small, "dp", axis=0)
-        return full, unpack_rows(small_full, lengths)
-    *gathered, small_full = gather_all([*matrices, small], devices)
-    full = [g.reshape(devices * m.shape[0], m.shape[1]) for g, m in zip(gathered, matrices)]
-    return full, unpack_rows(small_full.reshape(devices, SMALL_ROWS, LANES), lengths)
+    full = [lax.all_gather(m, "dp", axis=0, tiled=True) for m in matrices]
+    small_full = lax.all_gather(small, "dp", axis=0)
+    return full, unpack_rows(small_full, lengths)
 
 
 def scatter_grads(matrices, vectors, devices):
     lengths = [v.shape[0] // devices for v in vectors]
     small = pack_rows(vectors, devices, jnp.float32)
-    if devices > 32:
-        owned = [lax.psum_scatter(m, "dp", scatter_dimension=0, tiled=True) for m in matrices]
-        small_owned = lax.psum_scatter(small, "dp", scatter_dimension=0, tiled=True)[0]
-    else:
-        chips = devices // 2
-        low = [to_low(m).reshape(chips, 2, m.shape[0] // devices, m.shape[1]) for m in matrices]
-        small = small.reshape(chips, 2, SMALL_ROWS, LANES)
-        *owned, small_owned = scatter_all([*low, small], devices)
+    owned = [lax.psum_scatter(m, "dp", scatter_dimension=0, tiled=True) for m in matrices]
+    small_owned = lax.psum_scatter(small, "dp", scatter_dimension=0, tiled=True)[0]
     return owned, [small_owned[j, :n] for j, n in enumerate(lengths)]
 
 
@@ -375,6 +703,25 @@
     heads = width // HEAD_DIM
     scale = HEAD_DIM ** (-0.5)
     devices = lax.axis_size("dp")
+    if qkv_weight.shape[0] % 8 == 0:
+        return whole_layer(
+            tokens,
+            lengths,
+            (qkv_weight, out_weight, ff_in_weight, ff_out_weight),
+            (
+                query_bias,
+                value_bias,
+                out_bias,
+                norm_one_gain,
+                norm_one_shift,
+                ff_out_bias,
+                norm_two_gain,
+                norm_two_shift,
+                ff_in_bias,
+            ),
+            out_grad,
+            devices,
+        )
     (weight_qkv, weight_out, weight_in, weight_down), vectors = gather_params(
         (qkv_weight, out_weight, ff_in_weight, ff_out_weight),
         (

time: 290 us -> 169 us (0.58)
  matrix products: 41.3 us -> 0 us
  Pallas kernels: 207 us -> 168 us
  local copies, waits for them, and re-layouts: 29.4 us -> 0 us
  other arithmetic: 10.1 us -> 0 us
    dot_general x18 -> x0, matrix products: 41.3 us -> none  [the longest x4 15.4 us: matmul(): return jnp.dot(left, right, preferred_element_type=jnp.float32)]
    pallas_call x2, Pallas kernels: 207 us -> 168 us  [the longest x1 165 us: whole_layer(): pl.pallas_call(kernel, out_shape=out_list, in_specs=[smem if a is lengths...]
    unnamed x82 -> x0, local copies, waits for them, and re-layouts: 9.88 us -> none
    reduce_sum x10 -> x0, other arithmetic: 6.39 us -> none  [the longest x2 2.26 us: layer_norm(): centered = hidden - center]
    pad x18 -> x0, local copies, waits for them, and re-layouts: 6.02 us -> none  [pack_rows(): rows.append(jnp.pad(piece, ((0, 0), (0, 0), (0, LANES - piece.shape[2]))))]
    convert_element_type x10 -> x0, local copies, waits for them, and re-layouts: 5.03 us -> none  [the longest x9 3.95 us: as_float(): return values.astype(jnp.float32)]
where the time goes in v2:
time: 169 us
  Pallas kernels  168 us (99%)
    pallas_call x1, Pallas kernels, whole_layer(): pl.pallas_call(kernel, out_shape=out_list, in_specs=[smem if a is lengths...  165 us

profile of v2, /device:TPU:0, one launch (start us, length us, event | category | flops | bytes accessed | tf_op | source)
XLA Modules:
  0.0 168.7 jit_solution(16956766346868016892)
XLA Ops:
  0.7 165.3 %encoder_layer.1 = (bf16[128,768]{1,0:T(8,128)(2,1)}, f32[128,768]{1,0:T(8,128)}, f32[24,2304]{1,0:T(8,128)}, f32[24,768]{1,0:T(8,128)}, f32[24,3072]{1,0:T(8,12...) custom-call(s32[2]{0:T(128)} %refs_0_.1, ...), custom_call_target="tpu_custom_call" | custom-call | tf_op jit(solution)/shard_map/encoder_layer/pallas_call | solution.py:589
  166.0 2.6 %publish.1 = (bf16[128,768]{1,0:T(8,128)(2,1)}, f32[128,768]{1,0:T(8,128)}, f32[24,2304]{1,0:T(8,128)}, f32[24,768]{1,0:T(8,128)}, f32[24,3072]{1,0:T(8,128)}, /...) custom-call(bf16[128,768]{1,0:T(8,128)(2,1)} %get-tuple-element.45.r, ...), custom_call_target="tpu_custom_call" | custom-call | tf_op jit(solution)/shard_map/publish/pallas_call | solution.py:599

commit v3 on v2

--- a/solution.py
+++ b/solution.py
@@ -64,6 +64,7 @@
 
 WEIGHTS = 4
 VECTORS = 9
+TURNED = (3,)
 CHUNK = 384
 
 
@@ -170,19 +171,21 @@
         v = ref.vector[j]
         pack[j : j + 1, 0 : v.shape[1]] = v[...].astype(jnp.float32)
     weights[WEIGHTS][own, core] = pack[...]
-    greet(place)
     for w in range(WEIGHTS):
         send(shards[w], raws[w], ref.raw_send.at[w], ref.raw_recv.at[w], sibling)
 
-    def pass_on(w, chip, da, ds, dt, to_s, to_t):
+    def pass_on(w, chip, da, ds, dt, to_a, to_s, to_t):
         part = block(weights[w], w, chip, core)
+        if to_a:
+            for d in range(1, depth):
+                send(part, part, ref.g_send_a.at[w, d - 1, ds], ref.g_recv_a.at[w, d - 1, ds], place.device(d, 0, 0))
+        if to_s:
+            for d in range(1, side):
+                send(part, part, ref.g_send_s.at[w, d - 1, da], ref.g_recv_s.at[w, d - 1, da], place.device(0, d, 0))
         if to_t:
             for d in range(1, side):
                 at = da * side + ds
                 send(part, part, ref.g_send_t.at[w, d - 1, at], ref.g_recv_t.at[w, d - 1, at], place.device(0, 0, d))
-        if to_s:
-            for d in range(1, side):
-                send(part, part, ref.g_send_s.at[w, d - 1, da], ref.g_recv_s.at[w, d - 1, da], place.device(0, d, 0))
         if (da, ds, dt) != (0, 0, 0) or w == WEIGHTS:
             at = (da * side + ds) * side + dt
             send(part, part, ref.g_send_c.at[w, at], ref.g_recv_c.at[w, at], sibling)
@@ -197,23 +200,21 @@
             half = both.shape[1] // 2
             weights[w][0, rows_of(w, own)] = both[:, :half]
             weights[w][1, rows_of(w, own)] = both[:, half:]
-        part = block(weights[w], w, own, core)
-        for d in range(1, depth):
-            send(part, part, ref.g_send_a.at[w, d - 1], ref.g_recv_a.at[w, d - 1], place.device(d, 0, 0))
-        pass_on(w, own, 0, 0, 0, True, True)
+        pass_on(w, own, 0, 0, 0, True, True, True)
 
     def gather_a(w):
         for da in range(1, depth):
-            chip = place.at(depth - da, 0, 0)
-            arrived(block(weights[w], w, chip, core), ref.g_recv_a.at[w, da - 1])
-            pass_on(w, chip, da, 0, 0, True, True)
+            for ds in range(side if w in TURNED else 1):
+                chip = place.at(depth - da, (side - ds) % side, 0)
+                arrived(block(weights[w], w, chip, core), ref.g_recv_a.at[w, da - 1, ds])
+                pass_on(w, chip, da, ds, 0, False, w not in TURNED, True)
 
     def gather_s(w):
-        for da in range(depth):
+        for da in range(1 if w in TURNED else depth):
             for ds in range(1, side):
                 chip = place.at((depth - da) % depth, side - ds, 0)
                 arrived(block(weights[w], w, chip, core), ref.g_recv_s.at[w, ds - 1, da])
-                pass_on(w, chip, da, ds, 0, False, True)
+                pass_on(w, chip, da, ds, 0, w in TURNED, False, True)
 
     def gather_t(w):
         for da in range(depth):
@@ -221,7 +222,7 @@
                 for dt in range(1, side):
                     chip = place.at((depth - da) % depth, (side - ds) % side, side - dt)
                     arrived(block(weights[w], w, chip, core), ref.g_recv_t.at[w, dt - 1, da * side + ds])
-                    pass_on(w, chip, da, ds, dt, False, False)
+                    pass_on(w, chip, da, ds, dt, False, False, False)
 
     def gather_c(w):
         for da in range(depth):
@@ -233,13 +234,16 @@
                     arrived(block(weights[w], w, chip, 1 - core),
                             ref.g_recv_c.at[w, (da * side + ds) * side + dt])
 
-    arrivals = (WEIGHTS, 0, 1, 2, 3)
-    for w in arrivals:
+    for w in (WEIGHTS, 0, 1, 2, 3):
         gather_own(w)
-    for w in arrivals:
-        gather_a(w)
-    for w in arrivals:
-        gather_s(w)
+    gather_a(WEIGHTS)
+    gather_a(0)
+    gather_s(3)
+    gather_a(1)
+    gather_s(WEIGHTS)
+    gather_s(0)
+    gather_a(2)
+    gather_s(1)
 
     tokens = ref.tokens
     rows, width = tokens.shape
@@ -281,6 +285,7 @@
             at = h * half + c
             out = dot(tokens[...], weights[0][h, :, c : c + CHUNK]) + qkv_bias[:, at : at + CHUNK]
             qkv[:, at : at + CHUNK] = out.astype(jnp.bfloat16)
+    gather_s(2)
     for pair in range(heads // 2):
         found = []
         for h in (2 * pair, 2 * pair + 1):
@@ -292,6 +297,7 @@
             found.append(dot(weight.astype(jnp.bfloat16), v))
         at = pair * 2 * HEAD_DIM
         context[:, at : at + 2 * HEAD_DIM] = jnp.concatenate(found, axis=1).astype(jnp.bfloat16)
+    gather_a(3)
     ref.context_t[...] = context[...].T
 
     gather_t(1)
@@ -321,6 +327,7 @@
     down = jnp.concatenate([dot(ref.active[...], weights[3][h]) for h in range(2)], axis=1)
     unit_two, inverse_two = norm_parts(ref.first_norm[...] + down + bias_down)
     ref.encoded[...] = (unit_two * gain_second + shift_second).astype(jnp.bfloat16)
+    ref.ship(0)
 
     order = [(da, ds, dt) for dt in range(1, side) for ds in list(range(1, side)) + [0] for da in list(range(1, depth)) + [0]]
     order += [(da, ds, 0) for ds in range(1, side) for da in list(range(1, depth)) + [0]]
@@ -348,14 +355,14 @@
                 at = da * side + ds
                 arrived(from_t[w].at[d - 1, at], ref.s_recv_t.at[w, d - 1, at])
                 total = total + from_t[w][d - 1, at].astype(jnp.float32)
-            if ds == 0:
+            if ds == 0 and (da == 0 or w not in TURNED):
                 for d in range(1, side):
                     arrived(from_s[w].at[d - 1, da], ref.s_recv_s.at[w, d - 1, da])
                     total = total + from_s[w][d - 1, da].astype(jnp.float32)
-                if da == 0:
-                    for d in range(1, depth):
-                        arrived(from_a[w].at[d - 1], ref.s_recv_a.at[w, d - 1])
-                        total = total + from_a[w][d - 1].astype(jnp.float32)
+            if da == 0 and (ds == 0 or w in TURNED):
+                for d in range(1, depth):
+                    arrived(from_a[w].at[d - 1, ds], ref.s_recv_a.at[w, d - 1, ds])
+                    total = total + from_a[w][d - 1, ds].astype(jnp.float32)
         return chip, total
 
     def relay(w, da, ds, dt, target, ssem, rsem, device):
@@ -365,23 +372,26 @@
         send(slot, target, ssem, rsem, device)
 
     def scatter_t(w):
+        lines = [(da, ds) for ds in list(range(1, side)) + [0] for da in list(range(1, depth)) + [0]]
+        if w in TURNED:
+            lines = [(da, ds) for da in list(range(1, depth)) + [0] for ds in list(range(1, side)) + [0]]
         for dt in range(1, side):
-            for ds in list(range(1, side)) + [0]:
-                for da in list(range(1, depth)) + [0]:
-                    at = da * side + ds
-                    relay(w, da, ds, dt, from_t[w].at[dt - 1, at], ref.s_send_t.at[w, dt - 1, at],
-                          ref.s_recv_t.at[w, dt - 1, at], place.device(0, 0, dt))
+            for da, ds in lines:
+                at = da * side + ds
+                relay(w, da, ds, dt, from_t[w].at[dt - 1, at], ref.s_send_t.at[w, dt - 1, at],
+                      ref.s_recv_t.at[w, dt - 1, at], place.device(0, 0, dt))
 
     def scatter_s(w):
         for ds in range(1, side):
-            for da in list(range(1, depth)) + [0]:
+            for da in [0] if w in TURNED else list(range(1, depth)) + [0]:
                 relay(w, da, ds, 0, from_s[w].at[ds - 1, da], ref.s_send_s.at[w, ds - 1, da],
                       ref.s_recv_s.at[w, ds - 1, da], place.device(0, ds, 0))
 
-    def scatter_a(w):
-        for da in range(1, depth):
-            relay(w, da, 0, 0, from_a[w].at[da - 1], ref.s_send_a.at[w, da - 1],
-                  ref.s_recv_a.at[w, da - 1], place.device(da, 0, 0))
+    def scatter_a(w, steps=None):
+        for da in steps or range(1, depth):
+            for ds in list(range(1, side)) + [0] if w in TURNED else [0]:
+                relay(w, da, ds, 0, from_a[w].at[da - 1, ds], ref.s_send_a.at[w, da - 1, ds],
+                      ref.s_recv_a.at[w, da - 1, ds], place.device(da, 0, 0))
 
     def finish(w):
         total = collect(w, 0, 0, 0)[1]
@@ -430,6 +440,7 @@
             at = h * half_in + c
             grads[2][h, :, c : c + CHUNK] = dot(ref.first_t[...], ref.grad_pre[:, at : at + CHUNK]).astype(jnp.bfloat16)
     scatter_c(2)
+    scatter_a(3, range(1, 2))
     grad_first = ref.grad_second[...] + dot_nt(ref.grad_pre[:, :half_in], weights[2][0])
     grad_first = grad_first + dot_nt(ref.grad_pre[:, half_in:], weights[2][1])
     unit_one = ref.unit_one[...]
@@ -441,11 +452,11 @@
     ref.grad_attn[...] = grad_attn
     grad_bias_out = column_sum(grad_attn.astype(jnp.float32))
     scatter_t(2)
+    scatter_a(3, range(2, depth))
     half = weights[1].shape[2]
     for h in range(2):
         grads[1][h] = dot(ref.context_t[...], ref.grad_attn[:, h * half : (h + 1) * half]).astype(jnp.bfloat16)
     scatter_c(1)
-    scatter_s(3)
     back = dot_nt(ref.grad_attn[:, :half], weights[1][0]) + dot_nt(ref.grad_attn[:, half:], weights[1][1])
     ref.grad_context[...] = back.astype(jnp.bfloat16)
     for pair in range(heads // 2):
@@ -490,24 +501,28 @@
     small = jnp.where(row == VECTORS - 1, small_in.reshape(devices, 1, LANES), small.reshape(devices, SMALL_ROWS, LANES))
     grads[WEIGHTS][...] = small.reshape(chips, 2, SMALL_ROWS, LANES)
     scatter_c(WEIGHTS)
-    scatter_s(2)
     scatter_t(0)
     scatter_t(WEIGHTS)
+    scatter_s(2)
     half = weights[0].shape[2]
     grad_tokens = ref.grad_first_sum[...] + dot_nt(ref.grad_qkv[:, :half], weights[0][0])
     ref.grad_tokens[...] = grad_tokens + dot_nt(ref.grad_qkv[:, half:], weights[0][1])
-    scatter_a(3)
+    ref.ship(1)
+    scatter_a(2)
     scatter_s(1)
-    scatter_a(2)
+    scatter_a(1)
+    scatter_s(3)
     scatter_s(0)
     scatter_s(WEIGHTS)
-    scatter_a(1)
     scatter_a(0)
     scatter_a(WEIGHTS)
     for w in (3, 2, 1, 0, WEIGHTS):
         finish(w)
+    for j in range(VECTORS):
+        ref.ship(2 + WEIGHTS + j)
     for w in (3, 2, 1, 0):
         put_out(w)
+        ref.ship(2 + w)
     for copy in started:
         copy.wait_send()
 
@@ -551,7 +566,7 @@
         raw=[low(*m.shape) for m in matrices], weight=halves + [small], grad=halves + [small],
         held=held + [full(chips, SMALL_ROWS, LANES)],
         from_t=per_block(side - 1, depth * side), from_s=per_block(side - 1, depth),
-        from_a=per_block(depth - 1), final=pieces, leave=pieces, enter=pieces,
+        from_a=per_block(depth - 1, side), final=pieces, leave=pieces, enter=pieces,
         pack=full(SMALL_ROWS, LANES),
         context=low(rows, width), first_low=low(rows, width), grad_ff=low(rows, width),
         grad_attn=low(rows, width), grad_context=low(rows, width),
@@ -561,7 +576,7 @@
         qkv=low(rows, 3 * width), grad_qkv=low(rows, 3 * width),
         active=low(rows, hidden), grad_pre=low(rows, hidden), active_t=low(hidden, rows),
         slope=full(rows, hidden), attend=full(heads, rows, rows))
-    by_a, by_s, by_t = (count, depth - 1), (count, side - 1, depth), (count, side - 1, depth * side)
+    by_a, by_s, by_t = (count, depth - 1, side), (count, side - 1, depth), (count, side - 1, depth * side)
     by_c, by_w = (count, chips), (WEIGHTS,)
     sems = dict(
         g_send_a=by_a, g_recv_a=by_a, s_send_a=by_a, s_recv_a=by_a,
@@ -571,6 +586,7 @@
         raw_send=by_w, raw_recv=by_w, f_send=by_w, f_recv=by_w)
     sems = {name: pltpu.SemaphoreType.DMA(shape) for name, shape in sems.items()}
     vmem = pl.BlockSpec(memory_space=pltpu.VMEM)
+    anywhere = pl.BlockSpec(memory_space=pl.ANY)
     smem = pl.BlockSpec(memory_space=pltpu.SMEM)
     arg_list, arg_tree = jax.tree.flatten(args)
     out_list, out_tree = jax.tree.flatten(outs)
@@ -579,19 +595,41 @@
     def kernel(*refs):
         cuts = [len(arg_list), len(arg_list) + len(out_list)]
         cuts.append(cuts[1] + len(scratch_list))
+        cuts += [cuts[2] + len(arg_list), cuts[2] + len(arg_list) + len(out_list)]
+        in_sems, out_sems = refs[-2:]
+        taken = list(refs[: cuts[0]])
+        loads = []
+        for i, source in enumerate(refs[: cuts[0]]):
+            if arg_list[i] is not lengths:
+                taken[i] = refs[cuts[2] + i]
+                loads.append(pltpu.make_async_copy(source, taken[i], in_sems.at[i]))
+                loads[-1].start()
+        made = refs[cuts[3] : cuts[4]]
+        leaving = []
+
+        def ship(i):
+            leaving.append(pltpu.make_async_copy(made[i], refs[cuts[0] + i], out_sems.at[i]))
+            leaving[-1].start()
+
         ref = SimpleNamespace(
-            **jax.tree.unflatten(arg_tree, refs[: cuts[0]]),
-            **jax.tree.unflatten(out_tree, refs[cuts[0] : cuts[1]]),
+            **jax.tree.unflatten(arg_tree, taken),
+            **jax.tree.unflatten(out_tree, made),
             **jax.tree.unflatten(scratch_tree, refs[cuts[1] : cuts[2]]),
-            **dict(zip(sems, refs[cuts[2] :])))
+            **dict(zip(sems, refs[cuts[4] : -2])), ship=ship)
+        greet(Place(devices))
+        for load in loads:
+            load.wait()
         layer_kernel(devices, ref)
+        for copy in leaving:
+            copy.wait()
 
     found = pl.pallas_call(
         kernel,
         out_shape=out_list,
-        in_specs=[smem if a is lengths else vmem for a in arg_list],
-        out_specs=[vmem] * len(out_list),
-        scratch_shapes=[pltpu.VMEM(s.shape, s.dtype) for s in scratch_list] + list(sems.values()),
+        in_specs=[smem if a is lengths else anywhere for a in arg_list],
+        out_specs=[anywhere] * len(out_list),
+        scratch_shapes=[pltpu.VMEM(s.shape, s.dtype) for s in [*scratch_list, *arg_list, *out_list]]
+        + list(sems.values()) + [pltpu.SemaphoreType.DMA((len(arg_list),)), pltpu.SemaphoreType.DMA((len(out_list),))],
         compiler_params=pltpu.CompilerParams(
             collective_id=0, has_side_effects=True, vmem_limit_bytes=VMEM_BYTES),
         name="encoder_layer",

time: 169 us -> 152 us (0.90)
  Pallas kernels: 168 us -> 151 us
    pallas_call x1, Pallas kernels: 165 us -> 148 us  [whole_layer(): pl.pallas_call(kernel, out_shape=out_list, in_specs=[smem if a is lengths...]
where the time goes in v3:
time: 152 us
  Pallas kernels  151 us (99%)
    pallas_call x1, Pallas kernels, whole_layer(): pl.pallas_call(kernel, out_shape=out_list, in_specs=[smem if a is lengths...  148 us

profile of v3, /device:TPU:0, one launch (start us, length us, event | category | flops | bytes accessed | tf_op | source)
XLA Modules:
  0.0 151.7 jit_solution(4889470889887983261)
XLA Ops:
  0.7 148.4 %encoder_layer.1 = (bf16[128,768]{1,0:T(8,128)(2,1)}, f32[128,768]{1,0:T(8,128)}, f32[24,2304]{1,0:T(8,128)}, f32[24,768]{1,0:T(8,128)}, f32[24,3072]{1,0:T(8,12...) custom-call(s32[2]{0:T(128)} %refs_0_.1, ...), custom_call_target="tpu_custom_call" | custom-call | tf_op jit(solution)/shard_map/encoder_layer/pallas_call | solution.py:626
  149.0 2.6 %publish.1 = (bf16[128,768]{1,0:T(8,128)(2,1)}, f32[128,768]{1,0:T(8,128)}, f32[24,2304]{1,0:T(8,128)}, f32[24,768]{1,0:T(8,128)}, f32[24,3072]{1,0:T(8,128)}, /...) custom-call(bf16[128,768]{1,0:T(8,128)(2,1)} %get-tuple-element.45.r, ...), custom_call_target="tpu_custom_call" | custom-call | tf_op jit(solution)/shard_map/publish/pallas_call | solution.py:637
